TPU v7x, 32 devices: a whole 2x2x4 slice. The times are simulated.
32 devices in a mesh: stn: 4 (over x, core), tm: 8 (over z, y).
Axes of the slice: x: 2, y: 2, z: 4, core: 2. Of those that a mesh axis runs over, the one named last changes fastest.
Arguments:
- samples: bfloat16 [2, 1024, 8, 20736], P(None, 'stn', 'tm'), may hold values from -22 to 22
- filter_taps: float32 [6, 3456], replicated, may hold values from -2.5 to 2.5
- station_flags: int32 [1024], P('stn'), may hold values 0 or 1
- channel_keep: int32 [3456], replicated, may hold values from 0 to 1, as said below
- beam_delay: int32 [64, 1024], replicated, may hold values from 0 to 3455
Outputs:
- visibilities: float32 [16, 2, 1024, 1024], P(None, None, 'stn', 'tm')
- beam_power: float32 [64, 3456], P('stn', 'tm')
Inputs may be any that keep to these rules, and one draw needn't show every extreme that they name: `channel_keep`: each value is 0 or 1, and the first fine channel of every output channel is 1.
All inputs are finite; a program needn't handle non-finite values. No bound on the sum of `station_flags` on one device may be relied on, other than what follows from the above.
Results may differ from a plain program's by a relative error of at most 0.013.
Values may be sent and summed in bfloat16 or wider, within the bound.
A program may use at most 128 MiB of HBM per device.

v0:
```python
import math

import jax
import jax.numpy as jnp
from jax import lax
from jax.sharding import PartitionSpec as P

INPUTS = 1024
FINE = 3456
OUTCH = 16
TAPS = 6


TRANSFORM_PRECISION = lax.Precision.HIGH


def phase_table(row_count, col_count, modulus):
    row_ids = lax.broadcasted_iota(jnp.int32, (row_count, col_count), 0)
    col_ids = lax.broadcasted_iota(jnp.int32, (row_count, col_count), 1)
    angles = (row_ids * col_ids % modulus).astype(jnp.float32) * (2.0 * math.pi / modulus)
    return (jnp.cos(angles), jnp.sin(angles))


def fine_spectra(samples, filter_taps, station_flags):
    inputs_dev = samples.shape[1]
    spec_dev = samples.shape[2]
    framed = samples.reshape(2, inputs_dev, spec_dev, TAPS, FINE)
    branch = jnp.sum(framed.astype(jnp.float32) * filter_taps[None, None, None], axis=3)
    fft_inner = 128
    fft_outer = FINE // fft_inner
    grid_view = branch.reshape(2, inputs_dev, spec_dev, fft_outer, fft_inner)
    cos_outer, sin_outer = phase_table(fft_outer, fft_outer, fft_outer)
    first_real = jnp.einsum(
        "kn,isnm->iskm", cos_outer, grid_view[0], precision=TRANSFORM_PRECISION
    ) + jnp.einsum("kn,isnm->iskm", sin_outer, grid_view[1], precision=TRANSFORM_PRECISION)
    first_imag = jnp.einsum(
        "kn,isnm->iskm", cos_outer, grid_view[1], precision=TRANSFORM_PRECISION
    ) - jnp.einsum("kn,isnm->iskm", sin_outer, grid_view[0], precision=TRANSFORM_PRECISION)
    cos_twist, sin_twist = phase_table(fft_outer, fft_inner, FINE)
    second_real = first_real * cos_twist + first_imag * sin_twist
    second_imag = first_imag * cos_twist - first_real * sin_twist
    cos_inner, sin_inner = phase_table(fft_inner, fft_inner, fft_inner)
    third_real = jnp.einsum(
        "qm,iskm->isqk", cos_inner, second_real, precision=TRANSFORM_PRECISION
    ) + jnp.einsum("qm,iskm->isqk", sin_inner, second_imag, precision=TRANSFORM_PRECISION)
    third_imag = jnp.einsum(
        "qm,iskm->isqk", cos_inner, second_imag, precision=TRANSFORM_PRECISION
    ) - jnp.einsum("qm,iskm->isqk", sin_inner, second_real, precision=TRANSFORM_PRECISION)
    factor = station_flags.astype(jnp.float32)[:, None, None] / math.sqrt(FINE)
    stacked = (
        jnp.stack(
            [
                third_real.reshape(inputs_dev, spec_dev, FINE),
                third_imag.reshape(inputs_dev, spec_dev, FINE),
            ]
        )
        * factor
    )
    return stacked.astype(jnp.bfloat16)


def beam_terms(delay_rows, incoming, fine_global):
    phase_turns = delay_rows[:, :, None] * fine_global[None, None, :] % FINE
    angles = phase_turns.astype(jnp.float32) * (2.0 * math.pi / FINE)
    weights = jnp.stack([jnp.cos(angles), jnp.sin(angles)]).astype(jnp.bfloat16)
    products = jnp.einsum("pbik,qitk->pqbtk", weights, incoming, preferred_element_type=jnp.float32)
    volt_real = products[0, 0] + products[1, 1]
    volt_imag = products[0, 1] - products[1, 0]
    return jnp.stack([volt_real, volt_imag])


def cross_products(left_data, right_data, local_count, sub_len):
    row_count = left_data.shape[1]
    col_count = right_data.shape[1]
    spec_count = left_data.shape[2]
    left_rows = left_data.reshape(2 * row_count, spec_count, local_count, sub_len)
    right_rows = right_data.reshape(2 * col_count, spec_count, local_count, sub_len)
    products = jnp.einsum(
        "atlg,btlg->lab", left_rows, right_rows, preferred_element_type=jnp.float32
    )
    vis_real = products[:, :row_count, :col_count] + products[:, row_count:, col_count:]
    vis_imag = products[:, row_count:, :col_count] - products[:, :row_count, col_count:]
    return jnp.stack([vis_real, vis_imag], axis=1)


def on_device(samples, filter_taps, station_flags, channel_keep, beam_delay):
    spectra = fine_spectra(samples, filter_taps, station_flags)
    turned = lax.all_to_all(spectra, "tm", split_axis=3, concat_axis=2, tiled=True)
    inputs_dev = turned.shape[1]
    spectra_all = turned.shape[2]
    fine_dev = turned.shape[3]
    group_len = FINE // OUTCH
    sub_len = min(group_len, fine_dev)
    local_count = fine_dev // sub_len
    tm_index = lax.axis_index("tm")
    stn_index = lax.axis_index("stn")
    fine_start = tm_index * fine_dev
    keep_local = lax.dynamic_slice_in_dim(channel_keep, fine_start, fine_dev, 0)
    keep_wide = keep_local.astype(jnp.bfloat16)
    fine_global = fine_start + jnp.arange(fine_dev, dtype=jnp.int32)
    masked = turned * keep_wide
    vis_local = cross_products(
        masked, lax.all_gather(turned, "stn", axis=1, tiled=True), local_count, sub_len
    )
    own_delays = lax.dynamic_slice_in_dim(beam_delay, stn_index * inputs_dev, inputs_dev, 1)
    voltages = lax.psum_scatter(
        beam_terms(own_delays, turned, fine_global).astype(jnp.bfloat16),
        "stn",
        scatter_dimension=1,
        tiled=True,
    ).astype(jnp.float32)
    beam_energy = jnp.sum(voltages[0] * voltages[0] + voltages[1] * voltages[1], axis=1)
    beam_power = beam_energy * keep_local.astype(jnp.float32) / (INPUTS * spectra_all)
    counts = jnp.sum(channel_keep.reshape(OUTCH, group_len), axis=1)
    first_channel = fine_start // group_len
    local_counts = lax.dynamic_slice_in_dim(counts, first_channel, local_count, 0)
    inv_scale = 1.0 / (local_counts.astype(jnp.float32) * spectra_all)
    scaled = vis_local * inv_scale[:, None, None, None]
    placed = lax.dynamic_update_slice_in_dim(
        jnp.zeros((OUTCH, 2, scaled.shape[2], INPUTS), jnp.float32), scaled, first_channel, 0
    )
    visibilities = lax.psum_scatter(
        placed.astype(jnp.bfloat16), "tm", scatter_dimension=3, tiled=True
    ).astype(jnp.float32)
    return (visibilities, beam_power)


def solution(mesh):
    return jax.shard_map(
        on_device,
        mesh=mesh,
        in_specs=(P(None, "stn", "tm", None), P(), P("stn"), P(), P()),
        out_specs=(P(None, None, "stn", "tm"), P("stn", "tm")),
        check_vma=False,
    )
```

profile of v0, /device:TPU:0, one launch (start us, length us, event | category | flops | bytes accessed | tf_op | source)
XLA Modules:
  0.0 849.8 jit_solution(14004677124410322033)
XLA Ops:
  7.3 28.2 %copy.75 = bf16[2,256,1,20736]{1,3,0,2:T(8,128)(2,1)} copy(bf16[2,256,1,20736]{3,1,2,0:T(8,128)(2,1)} %param.5) | data formatting | bytes 42467328 | tf_op args[0]
  35.5 17.1 %fusion = f32[2,256,3456]{1,2,0:T(8,128)} fusion(bf16[2,256,1,6,3456]{1,4,3,0,2:T(8,128)(2,1)} %bitcast.109, f32[6,3456]{1,0:T(8,128)S(1)} %copy-done.8), kind=kLoop, calls=%fused_computation.1 | loop fusion | flops 30081024 | bytes 28394496 | tf_op jit(solution)/shard_map/reduce_sum | solution.py:28
  52.6 6.4 fusion.122
  59.1 5.4 copy.77
  64.5 6.1 fusion.63
  70.6 5.6 copy.76
  76.3 4.4 fusion.65
  80.8 0.3 copy-done.6
  81.0 2.3 convolution_subtract_fusion
  83.3 3.5 fusion.11
  86.8 3.7 fusion.18
  90.5 5.6 fusion.16
  96.1 3.8 add_bitcast_fusion
  99.8 5.5 copy.82
  105.3 9.3 %copy.86 = f32[1,256,1,3456]{3,1,2,0:T(8,128)} copy(f32[1,256,1,3456]{1,0,3,2:T(1,128)} %bitcast.115) | data formatting | bytes 7077888 | tf_op jit(solution)/shard_map/stack | solution.py:51
  114.6 6.9 subtract_bitcast_fusion
  121.5 5.4 copy.85
  126.9 8.9 %copy.87 = f32[1,256,1,3456]{3,1,2,0:T(8,128)} copy(f32[1,256,1,3456]{1,0,3,2:T(1,128)} %bitcast.116) | data formatting | bytes 7077888 | tf_op jit(solution)/shard_map/stack | solution.py:51
  135.8 5.4 fusion.9
  141.3 9.8 %copy.88 = bf16[2,256,1,3456]{1,0,2,3:T(2,128)(2,1)} copy(bf16[2,256,1,3456]{3,1,2,0:T(8,128)(2,1)} %fusion.9) | data formatting | bytes 7077888 | tf_op jit(solution)/shard_map/convert_element_type | solution.py:59
  151.0 86.8 %all_to_all.15 = bf16[2,256,1,3456]{1,0,2,3:T(2,128)(2,1)S(1)} all-to-all(bf16[2,256,1,3456]{1,0,2,3:T(2,128)(2,1)} %copy.88), channel_id=1, replica_groups=mesh['stn'=4,'tm'=8] {'tm'}, dimensions={3} | all-to-all | bytes 7077888 | tf_op jit(solution)/shard_map/all_to_all | solution.py:88
  237.8 1.8 copy-done.4
  239.6 2.3 copy.89
  242.2 0.1 reduce_sum.28
  242.5 122.2 %cosine_convert_fusion = (bf16[1,64,256,432]{2,1,0,3:T(8,128)(2,1)}, bf16[1,64,256,432]{2,1,0,3:T(8,128)(2,1)}) fusion(s32[432]{0:T(512)S(1)} %iota_add_fusion, s32[64,256]{1,0:T(8,128)S(1)} %constant_dynamic-slice_fusion), kind=kLoop, calls=%fused_computation.10 | loop fusion | flops 77856768 | bytes 28378816 | tf_op jit(solution)/shard_map/convert.5
  364.7 27.3 %fusion.24 = f32[2,2,64,8,432]{2,3,0,1,4:T(8,128)} fusion(bf16[1,64,256,432]{2,1,0,3:T(8,128)(2,1)} %get-tuple-element.15, bf16[1,64,256,432]{2,1,0,3:T(8,128)(2,1)} %get-tuple-element.14, bf16[2,256,8,432,1]{1,3,2,0,4:T(8,128)(2,1)S(1)} %bitcast.114), kind=kOutput, calls=%fused_computation.40 | convolution fusion | flops 509607936 | bytes 35389440 | tf_op jit(solution)/shard_map/pbik,qitk->pqbtk/dot_general | solution.py:66
  392.0 2.2 fusion.37
  394.2 2.2 fusion.38
  396.4 0.4 pad_maximum_fusion
  396.8 3.1 copy.95
  400.0 9.2 %all_to_all.12 = bf16[512,8,2,216]{0,3,2,1:T(8,128)(2,1)} reshape(bf16[2,256,1,3456]{1,0,2,3:T(2,128)(2,1)} %copy-done.4) | data formatting | bytes 7077888 | tf_op jit(solution)/shard_map/all_to_all | solution.py:88
  409.2 26.5 %copy.90 = bf16[2,1024,8,432]{1,0,3,2:T(2,128)(2,1)} copy(bf16[2,1024,8,432]{1,3,2,0:T(8,128)(2,1)} %all-gather.2.cloned.1.call-done) | data formatting | bytes 28311552 | tf_op jit(solution)/shard_map/all_gather | solution.py:103
  435.7 23.7 %reshape.240 = bf16[2048,8,2,216]{0,3,2,1:T(8,128)(2,1)} reshape(bf16[2,1024,8,432]{1,0,3,2:T(2,128)(2,1)} %copy.90) | data formatting | bytes 28311552 | tf_op jit(solution)/shard_map/reshape | solution.py:77
  459.4 12.3 %convolution_bitcast_fusion = f32[2,512,2048]{2,1,0:T(8,128)S(1)} fusion(bf16[2048,8,2,216]{0,3,2,1:T(8,128)(2,1)} %reshape.240, bf16[512,8,2,216]{0,3,2,1:T(8,128)(2,1)} %all_to_all.12, bf16[2,216]{1,0:T(2,128)(2,1)S(1)} %mul.249), kind=kOutput, calls=%fused_computation.17 | convolution fusion | flops 7249526784 | bytes 26084192 | tf_op jit(solution)/shard_map/atlg,btlg->lab/dot_general | solution.py:78
  471.7 1.0 fusion.28
  472.7 6.0 broadcast_in_dim.2
  478.7 2.0 copy_dynamic-update-slice_fusion
  480.7 41.2 %copy.102 = bf16[16,2,256,1024]{2,1,0,3:T(2,128)(2,1)} copy(bf16[16,2,256,1024]{3,2,1,0:T(8,128)(2,1)} %copy_dynamic-update-slice_fusion) | data formatting | bytes 33554432
  521.9 27.6 %reshape.250 = bf16[1024,8192]{1,0:T(8,128)(2,1)} reshape(bf16[1024,16,2,256]{3,2,1,0:T(2,128)(2,1)} %bitcast.110) | data formatting | bytes 33554432
  549.6 1.0 convert_element_type.111
  550.6 0.1 fusion.40
  550.7 0.1 copy.104
  550.8 0.1 multiply_multiply_fusion
  551.0 0.7 copy.97
  551.7 279.4 %reduce-scatter.7.cloned.1.call-done = bf16[128,8192]{1,0:T(8,128)(2,1)} async-done(((bf16[1024,8192]{1,0:T(8,128)(2,1)}), bf16[128,8192]{1,0:T(8,128)(2,1)}) %reduce-scatter.7.cloned.1.call-update) | async-done | bytes 2097168
  831.0 4.5 reshape.251
  835.5 5.0 copy.103
  840.5 2.5 convert_element_type.109
  (36 shorter events, 0.7 us)
Async XLA Ops:
  7.2 235.3 %copy-start = (s32[64,1024]{1,0:T(8,128)S(1)}, s32[64,1024]{1,0:T(8,128)}, u32[]{:S(2)}) copy-start(s32[64,1024]{1,0:T(8,128)} %param.9) | copy-start | bytes 786436
  7.2 402.0 %all-gather.2.cloned.1.call-start = ((), (), s32[]{:S(2)}) async-start(), calls=%async_computation.3 | async-start | bytes 17694720 | tf_op jit(solution)/shard_map/all_gather | solution.py:103
  7.3 28.2 %copy-start.8 = (f32[6,3456]{1,0:T(8,128)S(1)}, f32[6,3456]{1,0:T(8,128)}, u32[]{:S(2)}) copy-start(f32[6,3456]{1,0:T(8,128)} %param.6) | copy-start | bytes 248836
  76.3 4.5 copy-start.3
  76.3 4.7 copy-start.6
  81.0 2.3 copy-start.2
  86.8 9.3 %copy-start.5 = (f32[256,27,128]{2,1,0:T(8,128)}, f32[256,27,128]{2,1,0:T(8,128)S(1)}, u32[]{:S(2)}) copy-start(f32[256,27,128]{2,1,0:T(8,128)S(1)} %get-tuple-element.8) | copy-start | bytes 10616836
  126.9 8.9 %copy-start.10 = (s32[256]{0:T(256)S(1)}, s32[256]{0:T(256)}, u32[]{:S(2)}) copy-start(s32[256]{0:T(256)} %param.7) | copy-start | bytes 3076
  237.8 1.8 copy-start.4
  239.6 2.4 copy-start.9
  241.9 307.7 %reduce-scatter.5.cloned.1.call-start = ((), (), s32[]{:S(2)}) async-start(), calls=%async_computation.4 | async-start | bytes 1310720 | tf_op jit(solution)/shard_map/reduce_scatter | solution.py:106
  242.4 122.2 %copy-start.7 = (bf16[2,256,1,3456]{1,3,0,2:T(8,128)(2,1)S(1)}, bf16[2,256,1,3456]{1,3,0,2:T(8,128)(2,1)}, u32[]{:S(2)}) copy-start(bf16[2,256,1,3456]{1,3,0,2:T(8,128)(2,1)} %copy.89) | copy-start | bytes 10616836
  400.0 431.1 %reduce-scatter.7.cloned.1.call-start = ((), (), s32[]{:S(2)}) async-start(), calls=%async_computation.5 | async-start | bytes 18874368
  835.5 7.5 copy-start.1
Sparse Core Ops, SparseCore 0:
  242.0 91.5 all-gather.1
  400.1 23.5 reduce-scatter.4
  549.7 281.3 reduce-scatter.6
where the time goes:
time: 858 us; the launch traced here: 850 us
  waiting for transfers between devices  279 us (33%)
  local copies, waits for them, and re-layouts  237 us (28%)
  other arithmetic  157 us (18%)
  blocking collectives  86.8 us (10%)
  matrix products  75.8 us (9%)
  between operations  14.2 us (2%)
    unnamed x4, waiting for transfers between devices  279 us
    another operation x1, other arithmetic  122 us
    unnamed x29, local copies, waits for them, and re-layouts  109 us
    all_to_all x1, blocking collectives, on_device(): lax.all_to_all(spectra, 'tm', split_axis=3, concat_axis=2, tiled=True)  86.8 us
    dot_general x1, matrix products, beam_terms(): jnp.einsum('pbik,qitk->pqbtk', weights, incoming, preferred_element_type=...  27.3 us
    all_gather x1, local copies, waits for them, and re-layouts, on_device(): lax.all_gather(turned, 'stn', axis=1, tiled=True)  26.5 us
    reshape x1, local copies, waits for them, and re-layouts, cross_products(): right_data.reshape(2 * col_count, spec_count, local_count, sub_len)  23.7 us
    another operation x2, local copies, waits for them, and re-layouts, fine_spectra(): jnp.stack([third_real.reshape(inputs_dev, spec_dev, FINE), third_imag.res...  18.2 us
  transfers between devices with their start and end apart: 3, of which 1 were waited for; matrix products, arithmetic and copies ran while one was open for 35% of the time, Pallas kernels for 0%

commit v1 on v0

v1 whole, which is shorter than its diff:
```python
import functools
import math

import jax
import jax.numpy as jnp
import numpy as np
from jax import lax
from jax.experimental import pallas as pl
from jax.experimental.pallas import tpu as pltpu
from jax.sharding import PartitionSpec as P

INPUTS = 1024
FINE = 3456
OUTCH = 16
TAPS = 6
R1 = 27
R2 = 128
LANES = 128
ROWS = 16


def cmul(a, w):
    (ar, ai), (wr, wi) = a, w
    return (ar * wr - ai * wi, ar * wi + ai * wr)


def unit(num, den):
    a = -2.0 * math.pi * (num % den) / den
    return (math.cos(a), math.sin(a))


def twist(a, num, den):
    if num % den == 0:
        return a
    return cmul(a, unit(num, den))


def dft3(x0, x1, x2):
    half_root3 = math.sqrt(3.0) / 2.0
    sr, si = x1[0] + x2[0], x1[1] + x2[1]
    dr, di = (x1[0] - x2[0]) * half_root3, (x1[1] - x2[1]) * half_root3
    mr, mi = x0[0] - 0.5 * sr, x0[1] - 0.5 * si
    return ((x0[0] + sr, x0[1] + si), (mr + di, mi - dr), (mr - di, mi + dr))


def dft9(x):
    inner = [dft3(x[f], x[3 + f], x[6 + f]) for f in range(3)]
    out = [None] * 9
    for g in range(3):
        res = dft3(*[twist(inner[f][g], f * g, 9) for f in range(3)])
        for h in range(3):
            out[g + 3 * h] = res[h]
    return out


def channelize_kernel(groups, per, x_ref, taps_ref, mat_ref, factor_ref, out_ref, mid_ref):
    step = pl.program_id(0)
    block_rows = x_ref.shape[1]

    def row_group(r, carry):
        rows = pl.ds(pl.multiple_of(r * ROWS, ROWS), ROWS)
        into = pl.ds(pl.multiple_of(step * block_rows + r * ROWS, ROWS), ROWS)

        def branch(n1):
            parts = []
            for part in range(2):
                total = None
                for p in range(TAPS):
                    at = p * FINE + n1 * R2
                    term = (
                        x_ref[part, rows, at : at + R2].astype(jnp.float32)
                        * taps_ref[p : p + 1, n1 * R2 : (n1 + 1) * R2]
                    )
                    total = term if total is None else total + term
                parts.append(total)
            return tuple(parts)

        first = [[None] * 9 for _ in range(3)]
        for b in range(9):
            res = dft3(branch(b), branch(9 + b), branch(18 + b))
            for c in range(3):
                first[c][b] = twist(res[c], b * c, 27)
        for c in range(3):
            res = dft9(first[c])
            for d in range(9):
                k1 = c + 3 * d
                mid_ref[k1, into, 0:R2] = res[d][0].astype(jnp.bfloat16)
                mid_ref[k1, into, R2 : 2 * R2] = res[d][1].astype(jnp.bfloat16)
        return carry

    lax.fori_loop(0, block_rows // ROWS, row_group, 0)

    @pl.when(step == pl.num_programs(0) - 1)
    def _():
        factor = factor_ref[...]

        def outer(k1, carry):
            res = lax.dot_general(
                mat_ref[k1],
                mid_ref[k1],
                (((1,), (1,)), ((), ())),
                preferred_element_type=jnp.float32,
            )
            res = (res * factor).astype(jnp.bfloat16)
            for og in range(groups):
                out_ref[og, k1] = res[og * 2 * per : (og + 1) * 2 * per]
            return carry

        lax.fori_loop(0, R1, outer, 0)


def transform_table(groups, per):
    k1 = np.arange(R1)[:, None, None]
    k2 = np.arange(R2)[None, :, None]
    n2 = np.arange(R2)[None, None, :]
    angle = 2.0 * np.pi * ((n2 * (k1 + R1 * k2)) % FINE) / FINE
    cos, sin = np.cos(angle), np.sin(angle)
    real_rows = np.concatenate([cos, sin], axis=2)
    imag_rows = np.concatenate([-sin, cos], axis=2)
    table = np.stack([real_rows, imag_rows], axis=1)
    table = table.reshape(R1, 2, groups, per, 2 * R2).transpose(0, 2, 1, 3, 4)
    return table.reshape(R1, 2 * R2, 2 * R2).astype(np.float32)


def channelize(samples, filter_taps, station_flags, channel_keep, groups, per):
    inputs_dev = samples.shape[1]
    x = samples.reshape(2, inputs_dev, TAPS * FINE)
    keep = channel_keep.reshape(R2, R1).T.reshape(R1, groups, 1, per)
    keep = jnp.broadcast_to(keep, (R1, groups, 2, per)).reshape(R1, 2 * R2, 1)
    table = jnp.asarray(transform_table(groups, per).astype(jnp.bfloat16))
    table = table * keep.astype(jnp.bfloat16)
    factor = (station_flags.astype(jnp.float32) / math.sqrt(FINE))[None, :]
    block = 32
    return pl.pallas_call(
        functools.partial(channelize_kernel, groups, per),
        grid=(inputs_dev // block,),
        in_specs=[
            pl.BlockSpec((2, block, TAPS * FINE), lambda i: (0, i, 0)),
            pl.BlockSpec((TAPS, FINE), lambda i: (0, 0)),
            pl.BlockSpec((R1, 2 * R2, 2 * R2), lambda i: (0, 0, 0)),
            pl.BlockSpec((1, inputs_dev), lambda i: (0, 0)),
        ],
        out_specs=pl.BlockSpec((groups, R1, 2 * per, inputs_dev), lambda i: (0, 0, 0, 0)),
        out_shape=jax.ShapeDtypeStruct((groups, R1, 2 * per, inputs_dev), jnp.bfloat16),
        scratch_shapes=[pltpu.VMEM((R1, inputs_dev, 2 * R2), jnp.bfloat16)],
        compiler_params=pltpu.CompilerParams(vmem_limit_bytes=48 << 20),
        name="channelize",
    )(x, filter_taps, table, factor)


def beam_kernel(per, x_ref, c1_ref, s1_ref, c2_ref, s2_ref, out_ref, w_ref):
    spec_count = x_ref.shape[0]
    inputs_dev = x_ref.shape[-1]
    beams = c1_ref.shape[1]
    cols = spec_count * 2 * per
    lane = lax.broadcasted_iota(jnp.int32, (beams, cols), 1)
    within = lane % per
    is_real = (lane % (2 * per)) < per

    def one(k1, carry):
        c1, s1 = c1_ref[k1], s1_ref[k1]
        for q in range(per):
            c2, s2 = c2_ref[q], s2_ref[q]
            w_ref[q * 2 * beams : q * 2 * beams + beams] = (c1 * c2 - s1 * s2).astype(jnp.bfloat16)
            w_ref[q * 2 * beams + beams : (q + 1) * 2 * beams] = (s1 * c2 + c1 * s2).astype(
                jnp.bfloat16
            )
        x = x_ref[:, 0, k1].reshape(cols, inputs_dev)
        prod = lax.dot_general(
            w_ref[...], x, (((1,), (1,)), ((), ())), preferred_element_type=jnp.float32
        )
        with_cos = prod[0:beams]
        with_sin = prod[beams : 2 * beams]
        for q in range(1, per):
            here = within == q
            with_cos = jnp.where(here, prod[q * 2 * beams : q * 2 * beams + beams], with_cos)
            with_sin = jnp.where(
                here, prod[q * 2 * beams + beams : (q + 1) * 2 * beams], with_sin
            )
        ahead = pltpu.roll(with_sin, cols - per, 1)
        behind = pltpu.roll(with_sin, per, 1)
        out_ref[0, k1] = (with_cos + jnp.where(is_real, ahead, -behind)).astype(jnp.bfloat16)
        return carry

    lax.fori_loop(0, R1, one, 0)


def beams_of(turned, delays, k2_start, local, per):
    spec_count, _, _, _, inputs_dev = turned.shape
    beams = delays.shape[0]
    cols = spec_count * 2 * per
    ids1 = jnp.arange(R1, dtype=jnp.int32)[:, None, None]
    ids2 = (k2_start + jnp.arange(local * per, dtype=jnp.int32))[:, None, None]
    ang1 = (delays[None] * ids1 % FINE).astype(jnp.float32) * (2.0 * math.pi / FINE)
    ang2 = (delays[None] * ids2 % R2).astype(jnp.float32) * (2.0 * math.pi / R2)
    small = pl.BlockSpec((R1, beams, inputs_dev), lambda o: (0, 0, 0))
    large = pl.BlockSpec((per, beams, inputs_dev), lambda o: (o, 0, 0))
    return pl.pallas_call(
        functools.partial(beam_kernel, per),
        grid=(local,),
        in_specs=[
            pl.BlockSpec((spec_count, 1, R1, 2 * per, inputs_dev), lambda o: (0, o, 0, 0, 0)),
            small,
            small,
            large,
            large,
        ],
        out_specs=pl.BlockSpec((1, R1, beams, cols), lambda o: (o, 0, 0, 0)),
        out_shape=jax.ShapeDtypeStruct((local, R1, beams, cols), jnp.bfloat16),
        scratch_shapes=[pltpu.VMEM((per * 2 * beams, inputs_dev), jnp.bfloat16)],
        compiler_params=pltpu.CompilerParams(vmem_limit_bytes=48 << 20),
        cost_estimate=pl.CostEstimate(
            flops=int(6e9), bytes_accessed=20 << 20, transcendentals=0
        ),
        name="beams",
    )(turned, jnp.cos(ang1), jnp.sin(ang1), jnp.cos(ang2), jnp.sin(ang2))


def left_kernel(per, x_ref, out_ref):
    inputs_dev = x_ref.shape[-1]
    depth = R1 * 2 * per
    x = x_ref[0, 0].reshape(depth, inputs_dev).astype(jnp.float32)
    pairs = x.reshape(R1, 2, per, inputs_dev)
    turned = jnp.concatenate([pairs[:, 1:], -pairs[:, :1]], axis=1).reshape(depth, inputs_dev)
    out_ref[0, 0, 0:inputs_dev] = x.T.astype(jnp.bfloat16)
    out_ref[0, 0, inputs_dev : 2 * inputs_dev] = turned.T.astype(jnp.bfloat16)


def left_of(turned, per):
    spec_count, local, _, _, inputs_dev = turned.shape
    depth = R1 * 2 * per
    return pl.pallas_call(
        functools.partial(left_kernel, per),
        grid=(local, spec_count),
        in_specs=[
            pl.BlockSpec((1, 1, R1, 2 * per, inputs_dev), lambda o, s: (s, o, 0, 0, 0)),
        ],
        out_specs=pl.BlockSpec((1, 1, 2 * inputs_dev, depth), lambda o, s: (o, s, 0, 0)),
        out_shape=jax.ShapeDtypeStruct((local, spec_count, 2 * inputs_dev, depth), jnp.bfloat16),
        compiler_params=pltpu.CompilerParams(vmem_limit_bytes=32 << 20),
        cost_estimate=pl.CostEstimate(flops=int(2e9), bytes_accessed=10 << 20, transcendentals=0),
        name="left_side",
    )(turned)


def correlate_kernel(scale_ref, left_ref, right_ref, out_ref):
    inputs_dev = right_ref.shape[-1]
    spec_count, depth = left_ref.shape[1], left_ref.shape[3]
    total = jnp.zeros((2 * inputs_dev, inputs_dev), jnp.float32)
    for s in range(spec_count):
        total = total + jnp.dot(
            left_ref[0, s],
            right_ref[0, s, 0].reshape(depth, inputs_dev),
            preferred_element_type=jnp.float32,
        )
    total = (total * scale_ref[pl.program_id(0)]).astype(jnp.bfloat16)
    for part in range(2):
        for h in range(inputs_dev // LANES):
            out_ref[h, 0, part] = total[
                part * inputs_dev : (part + 1) * inputs_dev, h * LANES : (h + 1) * LANES
            ]


def correlate(scale, left, right):
    count, spec_count, local, _, rows, inputs_dev = right.shape
    halves = inputs_dev // LANES
    depth = left.shape[3]
    return pl.pallas_call(
        correlate_kernel,
        grid=(local, count),
        in_specs=[
            pl.BlockSpec(memory_space=pltpu.SMEM),
            pl.BlockSpec((1, spec_count, 2 * inputs_dev, depth), lambda o, j: (o, 0, 0, 0)),
            pl.BlockSpec(
                (1, spec_count, 1, R1, rows, inputs_dev), lambda o, j: (j, 0, o, 0, 0, 0)
            ),
        ],
        out_specs=pl.BlockSpec(
            (halves, 1, 2, inputs_dev, LANES), lambda o, j: (j, o, 0, 0, 0)
        ),
        out_shape=jax.ShapeDtypeStruct(
            (count * halves, local, 2, inputs_dev, LANES), jnp.bfloat16
        ),
        compiler_params=pltpu.CompilerParams(vmem_limit_bytes=48 << 20),
        name="correlate",
    )(scale, left, right)


def on_device(stn_count, tm_count, samples, filter_taps, station_flags, channel_keep, beam_delay):
    inputs_dev = samples.shape[1]
    fine_dev = FINE // tm_count
    k2_dev = R2 // tm_count
    per = min(R2 // OUTCH, k2_dev)
    groups = R2 // per
    local = groups // tm_count
    spec_all = tm_count * samples.shape[2]
    tm_index = lax.axis_index("tm")
    stn_index = lax.axis_index("stn")

    spectra = channelize(samples, filter_taps, station_flags, channel_keep, groups, per)
    spectra = spectra.reshape(tm_count, local, R1, 2 * per, inputs_dev)
    turned = lax.all_to_all(spectra, "tm", 0, 0, tiled=True)
    gathered = lax.all_gather(turned, "stn", axis=0, tiled=False)

    own_delays = lax.dynamic_slice_in_dim(beam_delay, stn_index * inputs_dev, inputs_dev, 1)
    volts = beams_of(turned, own_delays, tm_index * k2_dev, local, per)
    left = left_of(turned, per)
    volts = lax.psum_scatter(volts, "stn", scatter_dimension=2, tiled=True).astype(jnp.float32)
    beams_dev = volts.shape[2]
    energy = jnp.sum(
        (volts * volts).reshape(local, R1, beams_dev, spec_all * 2, per), axis=3
    )
    energy = energy.transpose(2, 0, 3, 1).reshape(beams_dev, fine_dev)
    keep_local = lax.dynamic_slice_in_dim(channel_keep, tm_index * fine_dev, fine_dev, 0)
    beam_power = energy * keep_local.astype(jnp.float32) / (INPUTS * spec_all)

    counts = jnp.sum(channel_keep.reshape(OUTCH, FINE // OUTCH), axis=1)
    first = (tm_index * fine_dev) // (FINE // OUTCH)
    local_counts = lax.dynamic_slice_in_dim(counts, first, local, 0)
    scale = 1.0 / (local_counts.astype(jnp.float32) * spec_all)
    parts = correlate(scale, left, gathered)
    cols = INPUTS // tm_count
    if cols != LANES:
        parts = parts.reshape(-1, local, 2, inputs_dev, LANES // cols, cols)
        parts = parts.transpose(0, 4, 1, 2, 3, 5).reshape(-1, local, 2, inputs_dev, cols)
    swapped = lax.all_to_all(parts, "tm", 0, 0, tiled=True)
    swapped = swapped.reshape(OUTCH, -1, 2, inputs_dev, cols).astype(jnp.float32)
    visibilities = jnp.sum(swapped, axis=1)
    return (visibilities, beam_power)


def solution(mesh):
    return jax.shard_map(
        functools.partial(on_device, mesh.shape["stn"], mesh.shape["tm"]),
        mesh=mesh,
        in_specs=(P(None, "stn", "tm", None), P(), P("stn"), P(), P()),
        out_specs=(P(None, None, "stn", "tm"), P("stn", "tm")),
        check_vma=False,
    )
```

time: 858 us -> 306 us (0.36)
  local copies, waits for them, and re-layouts: 237 us -> 9.62 us
  waiting for transfers between devices: 279 us -> 103 us
  other arithmetic: 157 us -> 23.6 us
  matrix products: 75.8 us -> 0 us
  Pallas kernels: 0 us -> 62.3 us
    unnamed x4 -> x2, waiting for transfers between devices: 279 us -> 0.03 us
    another operation x3 -> x0, other arithmetic: 124 us -> none
    unnamed x29 -> x12, local copies, waits for them, and re-layouts: 109 us -> 7.08 us
    all_gather x1, waiting for transfers between devices: 0.01 us -> 79 us  [on_device(): gathered = lax.all_gather(turned, 'stn', axis=0, tiled=False)]
    dot_general x10 -> x0, matrix products: 75.8 us -> none  [the longest x1 27.3 us: beam_terms(): jnp.einsum('pbik,qitk->pqbtk', weights, incoming, preferred_element_type=...]
    pallas_call x0 -> x4, Pallas kernels: none -> 62.3 us  [the longest x1 23.9 us: beams_of(): pl.pallas_call(functools.partial(beam_kernel, per), grid=(local,), in_spe...]
    another operation x5 -> x0, local copies, waits for them, and re-layouts: 32.4 us -> none  [the longest x2 18.2 us: fine_spectra(): jnp.stack([third_real.reshape(inputs_dev, spec_dev, FINE), third_imag.res...]
    all_gather x1 -> x0, local copies, waits for them, and re-layouts: 26.5 us -> none  [on_device(): lax.all_gather(turned, 'stn', axis=1, tiled=True)]
  transfers between devices with their start and end apart: 3 -> 3, of which waited for: 1 -> 2; matrix products, arithmetic and copies ran while one was open for 35% -> 6% of each run, Pallas kernels for 0% -> 9%
where the time goes in v1:
time: 306 us; the launch traced here: 305 us
  waiting for transfers between devices  103 us (34%)
  blocking collectives  86.7 us (28%)
  Pallas kernels  62.3 us (20%)
  other arithmetic  23.6 us (8%)
  between operations  14.2 us (5%)
  local copies, waits for them, and re-layouts  9.62 us (3%)
  starting transfers between devices  5.59 us (2%)
    all_to_all x1, blocking collectives, on_device(): turned = lax.all_to_all(spectra, 'tm', 0, 0, tiled=True)  86.7 us
    all_gather x1, waiting for transfers between devices, on_device(): gathered = lax.all_gather(turned, 'stn', axis=0, tiled=False)  79 us
    reduce_scatter x1, waiting for transfers between devices, on_device(): lax.psum_scatter(volts, 'stn', scatter_dimension=2, tiled=True)  24.3 us
    pallas_call x1, Pallas kernels, beams_of(): pl.pallas_call(functools.partial(beam_kernel, per), grid=(local,), in_spe...  23.9 us
    pallas_call x1, Pallas kernels, channelize(): pl.pallas_call(functools.partial(channelize_kernel, groups, per), grid=(i...  19 us
    pallas_call x1, Pallas kernels, correlate(): pl.pallas_call(correlate_kernel, grid=(local, count), in_specs=[pl.BlockS...  15.9 us
    sin x1, other arithmetic, beams_of(): jnp.sin(ang1)  7.94 us
    unnamed x12, local copies, waits for them, and re-layouts  7.08 us
  transfers between devices with their start and end apart: 3, of which 2 were waited for; matrix products, arithmetic and copies ran while one was open for 6% of the time, Pallas kernels for 9%

profile of v1, /device:TPU:0, one launch (start us, length us, event | category | flops | bytes accessed | tf_op | source)
XLA Modules:
  0.0 305.4 jit_solution(15441856537148765940)
XLA Ops:
  7.2 0.0 copy-start
  7.2 0.0 all-gather.3.cloned.1.call-start
  7.2 0.7 convert_multiply_fusion.1
  7.9 0.7 convert_element_type.49
  8.7 0.2 convert_element_type.50
  8.9 0.1 copy.15
  9.0 0.0 copy-start.4
  9.0 3.8 %broadcast_multiply_fusion.mat_ref = bf16[27,256,256]{2,1,0:T(8,128)(2,1)} fusion(bf16[27,256,256]{2,1,0:T(8,128)(2,1)} %constant.71.clone, bf16[27,256]{1,0:T(8,128)(2,1)S(1)} %copy.15), kind=kLoop, calls=%fused_computation.13 | loop fusion | flops 1769472 | bytes 7091712 | tf_op jit(solution)/shard_map/mul | solution.py:131
  12.9 0.0 copy-done.4
  12.9 19.0 %channelize.1 = bf16[16,27,16,256]{3,2,1,0:T(8,128)(2,1)S(1)} custom-call(bf16[2,256,20736]{2,1,0:T(8,128)(2,1)} %bitcast.18, f32[6,3456]{1,0:T(8,128)S(1)} %copy-done.4, bf16[27,256,256]{2,1,0:T(8,128)(2,1)} %broadcast_multiply_fusion.mat_ref, f32[1,256]{1,0:T(1,128)S(1)} %bitcast.17), custom_call_target="tpu_custom_call" | custom-call | tf_op jit(solution)/shard_map/channelize/pallas_call | solution.py:134
  31.9 86.7 %all_to_all.10.x_ref = bf16[8,2,27,16,256]{4,3,2,1,0:T(8,128)(2,1)} all-to-all(bf16[8,2,27,16,256]{4,3,2,1,0:T(8,128)(2,1)S(1)} %bitcast.16), channel_id=1, replica_groups=mesh['stn'=4,'tm'=8] {'tm'}, dimensions={0} | all-to-all | bytes 7077888 | tf_op jit(solution)/shard_map/all_to_all | solution.py:302
  118.6 0.0 copy-start.5
  118.6 0.0 all-gather.3.cloned.1.call-update
  118.7 0.7 copy-done.5
  119.3 0.1 reshape.47
  119.4 0.1 reduce_sum.16
  119.5 0.1 multiply_divide_fusion.scale_ref
  119.6 0.0 copy-done
  119.6 0.0 copy-start.3
  119.6 2.0 copy-done.3
  121.6 3.4 %left_side.1.left_ref = bf16[2,8,512,432]{3,2,1,0:T(8,128)(2,1)S(1)} custom-call(bf16[8,2,27,16,256]{4,3,2,1,0:T(8,128)(2,1)S(1)} %copy-done.3), custom_call_target="tpu_custom_call" | custom-call | flops 2000000000 | bytes 10485760 | tf_op jit(solution)/shard_map/left_side/pallas_call | solution.py:232
  125.1 0.0 copy-start.2
  125.1 4.4 %copy-done.2 = bf16[2,8,512,432]{3,2,1,0:T(8,128)(2,1)} copy-done((bf16[2,8,512,432]{3,2,1,0:T(8,128)(2,1)}, bf16[2,8,512,432]{3,2,1,0:T(8,128)(2,1)S(1)}, u32[]{:S(2)}) %copy-start.2) | copy-done | bytes 7077912
  129.5 79.0 %all-gather.3.cloned.1.call-done = bf16[32,2,27,16,256]{4,3,2,1,0:T(8,128)(2,1)} async-done(((bf16[8,2,27,16,256]{4,3,2,1,0:T(8,128)(2,1)}), bf16[32,2,27,16,256]{4,3,2,1,0:T(8,128)(2,1)}) %all-gather.3.cloned.1.call-update) | async-done | bytes 14155792 | tf_op jit(solution)/shard_map/all_gather | solution.py:303
  208.5 15.9 %correlate.1 = bf16[8,2,2,256,128]{4,3,2,1,0:T(8,128)(2,1)} custom-call(f32[2]{0:T(128)S(1)} %multiply_divide_fusion.scale_ref, bf16[2,8,512,432]{3,2,1,0:T(8,128)(2,1)} %copy-done.2, bf16[4,8,2,27,16,256]{5,4,3,2,1,0:T(8,128)(2,1)} %bitcast.19), custom_call_target="tpu_custom_call" | custom-call | tf_op jit(solution)/shard_map/correlate/pallas_call | solution.py:268
  224.4 5.5 %all-to-all-start.1 = ((bf16[8,2,2,256,128]{4,3,2,1,0:T(8,128)(2,1)}), bf16[8,2,2,256,128]{4,3,2,1,0:T(8,128)(2,1)S(1)}, u32[]{:S(2)}, u32[]{:S(2)}) async-start(bf16[8,2,2,256,128]{4,3,2,1,0:T(8,128)(2,1)} %correlate.1), calls=%async_computation.1 | async-start | bytes 4194304 | tf_op jit(solution)/shard_map/all_to_all | solution.py:326
  229.9 0.0 reduce-scatter.2.cloned.1.call-start
  230.0 4.1 %fusion.10 = (f32[16,64,256]{2,1,0:T(8,128)S(1)}, f32[16,64,256]{2,1,0:T(8,128)S(1)}) fusion(s32[16]{0:T(128)S(1)} %iota_add_fusion, s32[64,256]{1,0:T(8,128)S(1)} %constant_dynamic-slice_fusion), kind=kLoop, calls=%fused_computation.20 | loop fusion | flops 3670016 | bytes 2162752 | tf_op jit(solution)/shard_map/sin | solution.py:216
  234.1 7.9 %fusion.4 = (f32[27,64,256]{2,1,0:T(8,128)}, f32[27,64,256]{2,1,0:T(8,128)S(1)}) fusion(s32[64,256]{1,0:T(8,128)S(1)} %constant_dynamic-slice_fusion), kind=kLoop, calls=%fused_computation.11 | loop fusion | flops 3981312 | bytes 3604480 | tf_op jit(solution)/shard_map/sin | solution.py:216
  242.1 23.9 %beams.1 = bf16[2,27,64,128]{3,2,1,0:T(8,128)(2,1)} custom-call(bf16[8,2,27,16,256]{4,3,2,1,0:T(8,128)(2,1)} %all_to_all.10.x_ref, f32[27,64,256]{2,1,0:T(8,128)S(1)} %get-tuple-element.5.c1_ref, f32[27,64,256]{2,1,0:T(8,128)} %get-tuple-element.4.s1_ref, f32[16,64,256]{2,1,0:T(8,128)S(1)} %get-tuple-element.3.c2_ref, f32[16,64,256]{2,1,0:T(8,128)S(1)} %get-tuple-element.2.s2_ref), custom_call_target="tpu_custom_call" | custom-call | flops 6000000000 | bytes 20971520 | tf_op jit(solution)/shard_map/beams/pallas_call | solution.py:198
  266.0 0.0 reduce-scatter.2.cloned.1.call-update
  266.0 0.1 dynamic-slice_convert_fusion
  266.1 24.3 %reduce-scatter.2.cloned.1.call-done = bf16[2,27,16,128]{3,2,1,0:T(8,128)(2,1)} async-done(((bf16[2,27,64,128]{3,2,1,0:T(8,128)(2,1)}), bf16[2,27,16,128]{3,2,1,0:T(8,128)(2,1)}) %reduce-scatter.2.cloned.1.call-update) | async-done | bytes 221200 | tf_op jit(solution)/shard_map/reduce_scatter | solution.py:308
  290.4 1.0 convert_multiply_fusion
  291.4 2.0 copy.16
  293.4 1.8 bitcast_reduce_fusion
  295.2 0.1 reshape.51
  295.3 0.0 copy-start.1
  295.3 0.6 multiply_multiply_fusion
  295.9 0.0 all-to-all-done.1
  295.9 2.6 bitcast_convert_fusion
  298.6 0.0 copy-done.1
  (4 shorter events, 0.0 us)
Async XLA Ops:
  7.2 112.5 %copy-start = (s32[64,1024]{1,0:T(8,128)S(1)}, s32[64,1024]{1,0:T(8,128)}, u32[]{:S(2)}) copy-start(s32[64,1024]{1,0:T(8,128)} %param.10) | copy-start | bytes 786436
  7.2 201.3 %all-gather.3.cloned.1.call-start = ((), (), s32[]{:S(2)}) async-start(), calls=%async_computation.4 | async-start | bytes 17694720 | tf_op jit(solution)/shard_map/all_gather | solution.py:303
  9.0 3.9 %copy-start.4 = (f32[6,3456]{1,0:T(8,128)S(1)}, f32[6,3456]{1,0:T(8,128)}, u32[]{:S(2)}) copy-start(f32[6,3456]{1,0:T(8,128)} %taps_ref.1) | copy-start | bytes 248836
  118.6 0.7 copy-start.5
  119.6 2.0 copy-start.3
  125.1 4.4 %copy-start.2 = (bf16[2,8,512,432]{3,2,1,0:T(8,128)(2,1)}, bf16[2,8,512,432]{3,2,1,0:T(8,128)(2,1)S(1)}, u32[]{:S(2)}) copy-start(bf16[2,8,512,432]{3,2,1,0:T(8,128)(2,1)S(1)} %left_side.1.left_ref) | copy-start | bytes 21233668
  224.4 71.5 %all-to-all-start.1 = ((bf16[8,2,2,256,128]{4,3,2,1,0:T(8,128)(2,1)}), bf16[8,2,2,256,128]{4,3,2,1,0:T(8,128)(2,1)S(1)}, u32[]{:S(2)}, u32[]{:S(2)}) async-start(bf16[8,2,2,256,128]{4,3,2,1,0:T(8,128)(2,1)} %correlate.1), calls=%async_computation.1 | async-start | bytes 4194304 | tf_op jit(solution)/shard_map/all_to_all | solution.py:326
  229.9 60.5 %reduce-scatter.2.cloned.1.call-start = ((), (), s32[]{:S(2)}) async-start(), calls=%async_computation.3 | async-start | bytes 1105920 | tf_op jit(solution)/shard_map/reduce_scatter | solution.py:308
  295.3 3.3 %copy-start.1 = (s32[64,1024]{1,0:T(8,128)S(1)}, s32[64,1024]{1,0:T(8,128)}, u32[]{:S(2)}) copy-start(s32[64,1024]{1,0:T(8,128)} %param.10) | copy-start | bytes 786436
Sparse Core Ops, SparseCore 0:
  118.7 89.7 all-gather.2
  266.2 24.2 reduce-scatter.1

commit v2 on v1

--- a/solution.py
+++ b/solution.py
@@ -53,7 +53,8 @@
     return out
 
 
-def channelize_kernel(groups, per, x_ref, taps_ref, mat_ref, factor_ref, out_ref, mid_ref):
+def channelize_kernel(groups, per, local, x_ref, taps_ref, mat_ref, factor_ref, *rest):
+    out_refs, mid_ref = rest[:local], rest[local]
     step = pl.program_id(0)
     block_rows = x_ref.shape[1]
 
@@ -103,7 +104,7 @@
             )
             res = (res * factor).astype(jnp.bfloat16)
             for og in range(groups):
-                out_ref[og, k1] = res[og * 2 * per : (og + 1) * 2 * per]
+                out_refs[og % local][og // local, k1] = res[og * 2 * per : (og + 1) * 2 * per]
             return carry
 
         lax.fori_loop(0, R1, outer, 0)
@@ -122,7 +123,7 @@
     return table.reshape(R1, 2 * R2, 2 * R2).astype(np.float32)
 
 
-def channelize(samples, filter_taps, station_flags, channel_keep, groups, per):
+def channelize(samples, filter_taps, station_flags, channel_keep, groups, per, local):
     inputs_dev = samples.shape[1]
     x = samples.reshape(2, inputs_dev, TAPS * FINE)
     keep = channel_keep.reshape(R2, R1).T.reshape(R1, groups, 1, per)
@@ -132,7 +133,7 @@
     factor = (station_flags.astype(jnp.float32) / math.sqrt(FINE))[None, :]
     block = 32
     return pl.pallas_call(
-        functools.partial(channelize_kernel, groups, per),
+        functools.partial(channelize_kernel, groups, per, local),
         grid=(inputs_dev // block,),
         in_specs=[
             pl.BlockSpec((2, block, TAPS * FINE), lambda i: (0, i, 0)),
@@ -140,8 +141,14 @@
             pl.BlockSpec((R1, 2 * R2, 2 * R2), lambda i: (0, 0, 0)),
             pl.BlockSpec((1, inputs_dev), lambda i: (0, 0)),
         ],
-        out_specs=pl.BlockSpec((groups, R1, 2 * per, inputs_dev), lambda i: (0, 0, 0, 0)),
-        out_shape=jax.ShapeDtypeStruct((groups, R1, 2 * per, inputs_dev), jnp.bfloat16),
+        out_specs=[
+            pl.BlockSpec((groups // local, R1, 2 * per, inputs_dev), lambda i: (0, 0, 0, 0))
+        ]
+        * local,
+        out_shape=[
+            jax.ShapeDtypeStruct((groups // local, R1, 2 * per, inputs_dev), jnp.bfloat16)
+        ]
+        * local,
         scratch_shapes=[pltpu.VMEM((R1, inputs_dev, 2 * R2), jnp.bfloat16)],
         compiler_params=pltpu.CompilerParams(vmem_limit_bytes=48 << 20),
         name="channelize",
@@ -286,6 +293,25 @@
     )(scale, left, right)
 
 
+def widen_kernel(*refs):
+    out_ref = refs[-1]
+    for o, ref in enumerate(refs[:-1]):
+        out_ref[o] = ref[0].astype(jnp.float32)
+
+
+def widen(parts):
+    count, _, rows, cols = parts[0].shape
+    local = len(parts)
+    return pl.pallas_call(
+        widen_kernel,
+        grid=(count,),
+        in_specs=[pl.BlockSpec((1, 2, rows, cols), lambda i: (i, 0, 0, 0))] * local,
+        out_specs=pl.BlockSpec((local, 2, rows, cols), lambda i: (i, 0, 0, 0)),
+        out_shape=jax.ShapeDtypeStruct((count * local, 2, rows, cols), jnp.float32),
+        name="widen",
+    )(*parts)
+
+
 def on_device(stn_count, tm_count, samples, filter_taps, station_flags, channel_keep, beam_delay):
     inputs_dev = samples.shape[1]
     fine_dev = FINE // tm_count
@@ -297,14 +323,38 @@
     tm_index = lax.axis_index("tm")
     stn_index = lax.axis_index("stn")
 
-    spectra = channelize(samples, filter_taps, station_flags, channel_keep, groups, per)
-    spectra = spectra.reshape(tm_count, local, R1, 2 * per, inputs_dev)
-    turned = lax.all_to_all(spectra, "tm", 0, 0, tiled=True)
-    gathered = lax.all_gather(turned, "stn", axis=0, tiled=False)
-
+    spectra = channelize(
+        samples, filter_taps, station_flags, channel_keep, groups, per, local
+    )
     own_delays = lax.dynamic_slice_in_dim(beam_delay, stn_index * inputs_dev, inputs_dev, 1)
-    volts = beams_of(turned, own_delays, tm_index * k2_dev, local, per)
-    left = left_of(turned, per)
+    counts = jnp.sum(channel_keep.reshape(OUTCH, FINE // OUTCH), axis=1)
+    first = (tm_index * fine_dev) // (FINE // OUTCH)
+    local_counts = lax.dynamic_slice_in_dim(counts, first, local, 0)
+    scale = 1.0 / (local_counts.astype(jnp.float32) * spec_all)
+    cols = INPUTS // tm_count
+
+    turned, gathered, volts, vis = [], [], [], []
+    for o in range(local):
+        turned.append(lax.all_to_all(spectra[o][:, None], "tm", 0, 0, tiled=True))
+        gathered.append(lax.all_gather(turned[o], "stn", axis=0, tiled=False))
+    for o in range(local):
+        left = left_of(turned[o], per)
+        volts.append(
+            beams_of(turned[o], own_delays, tm_index * k2_dev + o * per, 1, per)
+        )
+        parts = correlate(scale[o : o + 1], left, gathered[o])
+        if cols != LANES:
+            parts = parts.reshape(-1, 2, inputs_dev, LANES // cols, cols)
+            parts = parts.transpose(0, 3, 1, 2, 4)
+        parts = parts.reshape(tm_count, 2, inputs_dev, cols)
+        vis.append(lax.all_to_all(parts, "tm", 0, 0, tiled=True))
+    if tm_count * local == OUTCH and cols == LANES:
+        visibilities = widen(vis)
+    else:
+        swapped = jnp.stack(vis, axis=1).reshape(OUTCH, -1, 2, inputs_dev, cols)
+        visibilities = jnp.sum(swapped.astype(jnp.float32), axis=1)
+
+    volts = jnp.concatenate(volts, axis=0)
     volts = lax.psum_scatter(volts, "stn", scatter_dimension=2, tiled=True).astype(jnp.float32)
     beams_dev = volts.shape[2]
     energy = jnp.sum(
@@ -313,19 +363,6 @@
     energy = energy.transpose(2, 0, 3, 1).reshape(beams_dev, fine_dev)
     keep_local = lax.dynamic_slice_in_dim(channel_keep, tm_index * fine_dev, fine_dev, 0)
     beam_power = energy * keep_local.astype(jnp.float32) / (INPUTS * spec_all)
-
-    counts = jnp.sum(channel_keep.reshape(OUTCH, FINE // OUTCH), axis=1)
-    first = (tm_index * fine_dev) // (FINE // OUTCH)
-    local_counts = lax.dynamic_slice_in_dim(counts, first, local, 0)
-    scale = 1.0 / (local_counts.astype(jnp.float32) * spec_all)
-    parts = correlate(scale, left, gathered)
-    cols = INPUTS // tm_count
-    if cols != LANES:
-        parts = parts.reshape(-1, local, 2, inputs_dev, LANES // cols, cols)
-        parts = parts.transpose(0, 4, 1, 2, 3, 5).reshape(-1, local, 2, inputs_dev, cols)
-    swapped = lax.all_to_all(parts, "tm", 0, 0, tiled=True)
-    swapped = swapped.reshape(OUTCH, -1, 2, inputs_dev, cols).astype(jnp.float32)
-    visibilities = jnp.sum(swapped, axis=1)
     return (visibilities, beam_power)
 
 

time: 306 us -> 248 us (0.81)
  waiting for transfers between devices: 103 us -> 20.5 us
  local copies, waits for them, and re-layouts: 9.62 us -> 17.7 us
  Pallas kernels: 62.3 us -> 68.6 us
  blocking collectives: 86.7 us -> 92.9 us
  starting transfers between devices: 5.59 us -> 10.4 us
    all_gather x1 -> x2, waiting for transfers between devices: 79 us -> 0.01 us  [on_device(): gathered.append(lax.all_gather(turned[o], 'stn', axis=0, tiled=False))]
    reduce_scatter x1, waiting for transfers between devices: 24.3 us -> 5.37 us  [on_device(): lax.psum_scatter(volts, 'stn', scatter_dimension=2, tiled=True)]
    all_to_all x1 -> x2, waiting for transfers between devices: 0.01 us -> 15.1 us  [on_device(): vis.append(lax.all_to_all(parts, 'tm', 0, 0, tiled=True))]
    unnamed x12 -> x34, local copies, waits for them, and re-layouts: 7.08 us -> 14.9 us
    all_to_all x1 -> x2, blocking collectives: 86.7 us -> 92.9 us  [on_device(): turned.append(lax.all_to_all(spectra[o][:, None], 'tm', 0, 0, tiled=True))]
    pallas_call x1 -> x2, Pallas kernels: 19 us -> 25.2 us  [the longest x1 19.1 us: channelize(): pl.pallas_call(functools.partial(channelize_kernel, groups, per, local),...]
    all_to_all x1 -> x2, starting transfers between devices: 5.52 us -> 10.3 us  [on_device(): vis.append(lax.all_to_all(parts, 'tm', 0, 0, tiled=True))]
    pallas_call x1 -> x2, Pallas kernels: 23.9 us -> 24.3 us  [beams_of(): pl.pallas_call(functools.partial(beam_kernel, per), grid=(local,), in_spe...]
  transfers between devices with their start and end apart: 3 -> 5, of which waited for: 2 -> 2; matrix products, arithmetic and copies ran while one was open for 6% -> 8% of each run, Pallas kernels for 9% -> 18%
where the time goes in v2:
time: 248 us; the launch traced here: 246 us
  blocking collectives  92.9 us (37%)
  Pallas kernels  68.6 us (28%)
  other arithmetic  22.4 us (9%)
  waiting for transfers between devices  20.5 us (8%)
  local copies, waits for them, and re-layouts  17.7 us (7%)
  between operations  14 us (6%)
  starting transfers between devices  10.4 us (4%)
    all_to_all x2, blocking collectives, on_device(): turned.append(lax.all_to_all(spectra[o][:, None], 'tm', 0, 0, tiled=True))  92.9 us
    pallas_call x2, Pallas kernels, beams_of(): pl.pallas_call(functools.partial(beam_kernel, per), grid=(local,), in_spe...  24.3 us
    pallas_call x1, Pallas kernels, channelize(): pl.pallas_call(functools.partial(channelize_kernel, groups, per, local),...  19.1 us
    pallas_call x2, Pallas kernels, correlate(): pl.pallas_call(correlate_kernel, grid=(local, count), in_specs=[pl.BlockS...  15.7 us
    all_to_all x2, waiting for transfers between devices, on_device(): vis.append(lax.all_to_all(parts, 'tm', 0, 0, tiled=True))  15.1 us
    unnamed x34, local copies, waits for them, and re-layouts  14.9 us
    all_to_all x2, starting transfers between devices, on_device(): vis.append(lax.all_to_all(parts, 'tm', 0, 0, tiled=True))  10.3 us
    sin x1, other arithmetic, beams_of(): jnp.sin(ang1)  7.99 us
  transfers between devices with their start and end apart: 5, of which 2 were waited for; matrix products, arithmetic and copies ran while one was open for 8% of the time, Pallas kernels for 18%

profile of v2, /device:TPU:0, one launch (start us, length us, event | category | flops | bytes accessed | tf_op | source)
XLA Modules:
  0.0 246.5 jit_solution(12316498291933418340)
XLA Ops:
  7.2 0.0 all-gather.7.cloned.1.call-start
  7.2 0.8 convert_element_type.44
  8.0 0.2 convert_element_type.45
  8.2 0.1 copy.19
  8.3 0.7 convert_multiply_fusion.1
  9.0 3.8 %broadcast_multiply_fusion.mat_ref = bf16[27,256,256]{2,1,0:T(8,128)(2,1)} fusion(bf16[27,256,256]{2,1,0:T(8,128)(2,1)} %constant.81.clone, bf16[27,256]{1,0:T(8,128)(2,1)S(1)} %copy.19), kind=kLoop, calls=%fused_computation.9 | loop fusion | flops 1769472 | bytes 7091712 | tf_op jit(solution)/shard_map/mul | solution.py:132
  12.8 19.1 %channelize.1 = (bf16[8,27,16,256]{3,2,1,0:T(8,128)(2,1)S(1)}, bf16[8,27,16,256]{3,2,1,0:T(8,128)(2,1)S(1)}) custom-call(bf16[2,256,20736]{2,1,0:T(8,128)(2,1)} %bitcast.21, f32[6,3456]{1,0:T(8,128)S(1)} %copy-done.14, bf16[27,256,256]{2,1,0:T(8,128)(2,1)} %broadcast_multiply_fusion.mat_ref, f32[1,256]{1,0:T(1,128)S(1)} %bitcast.20), custom_call_target="tpu_custom_call" | custom-call | tf_op jit(solution)/shard_map/channelize/pallas_call | solution.py:135
  31.9 48.5 %all_to_all.20.x_ref = bf16[8,1,27,16,256]{4,3,2,1,0:T(8,128)(2,1)} all-to-all(bf16[8,1,27,16,256]{4,3,2,1,0:T(8,128)(2,1)S(1)} %bitcast.19), channel_id=1, replica_groups=mesh['stn'=4,'tm'=8] {'tm'}, dimensions={0} | all-to-all | bytes 3538944 | tf_op jit(solution)/shard_map/all_to_all | solution.py:338
  80.4 0.0 all-gather.7.cloned.1.call-update
  80.4 0.0 all-gather.5.cloned.1.call-start
  80.5 44.5 %all_to_all.21.x_ref = bf16[8,1,27,16,256]{4,3,2,1,0:T(8,128)(2,1)} all-to-all(bf16[8,1,27,16,256]{4,3,2,1,0:T(8,128)(2,1)S(1)} %bitcast.18), channel_id=1, replica_groups=mesh['stn'=4,'tm'=8] {'tm'}, dimensions={0} | all-to-all | bytes 3538944 | tf_op jit(solution)/shard_map/all_to_all | solution.py:338
  124.9 0.0 all-gather.5.cloned.1.call-update
  125.0 0.7 copy-done.16
  125.6 0.1 reshape.46
  125.7 0.1 reduce_sum.18
  125.9 0.1 multiply_divide_fusion
  126.0 0.6 fusion.17
  126.6 5.2 %fusion.15 = (f32[8,64,256]{2,1,0:T(8,128)}, f32[8,64,256]{2,1,0:T(8,128)}, f32[8,64,256]{2,1,0:T(8,128)}, f32[8,64,256]{2,1,0:T(8,128)}) fusion(s32[8]{0:T(128)S(1)} %get-tuple-element.17, s32[64,256]{1,0:T(8,128)S(1)} %constant_dynamic-slice_fusion, s32[8]{0:T(128)S(1)} %get-tuple-element.16), kind=kLoop, calls=%fused_computation.31 | loop fusion | flops 3670016 | bytes 2162752 | tf_op jit(solution)/shard_map/sin | solution.py:223
  131.8 8.0 %fusion.4 = (f32[27,64,256]{2,1,0:T(8,128)}, f32[27,64,256]{2,1,0:T(8,128)}) fusion(s32[64,256]{1,0:T(8,128)S(1)} %constant_dynamic-slice_fusion), kind=kLoop, calls=%fused_computation.7 | loop fusion | flops 3981312 | bytes 3604480 | tf_op jit(solution)/shard_map/sin | solution.py:223
  139.8 1.7 left_side.3.left_ref
  141.5 2.2 copy-done.7
  143.8 2.2 copy-done.8
  145.9 7.4 %correlate.3 = bf16[8,1,2,256,128]{4,3,2,1,0:T(8,128)(2,1)S(1)} custom-call(f32[1]{0:T(128)} %get-tuple-element.14.scale_ref, bf16[1,8,512,432]{3,2,1,0:T(8,128)(2,1)S(1)} %copy-done.8, bf16[4,8,1,27,16,256]{5,4,3,2,1,0:T(8,128)(2,1)} %bitcast.23), custom_call_target="tpu_custom_call" | custom-call | tf_op jit(solution)/shard_map/correlate/pallas_call | solution.py:275
  153.4 1.0 copy-done.4
  154.4 4.4 %all-to-all-start.3 = ((bf16[8,2,256,128]{3,2,1,0:T(8,128)(2,1)}), bf16[8,2,256,128]{3,2,1,0:T(8,128)(2,1)}, u32[]{:S(2)}, u32[]{:S(2)}) async-start(bf16[8,2,256,128]{3,2,1,0:T(8,128)(2,1)} %bitcast.17), calls=%async_computation.3 | async-start | bytes 2097152 | tf_op jit(solution)/shard_map/all_to_all | solution.py:350
  158.8 0.0 reduce-scatter.2.cloned.1.call-start
  158.9 1.5 copy-done.9
  160.3 1.0 copy-done.12
  161.4 1.0 copy-done.13
  162.4 12.2 %beams.2 = bf16[1,27,64,128]{3,2,1,0:T(8,128)(2,1)S(1)} custom-call(bf16[8,1,27,16,256]{4,3,2,1,0:T(8,128)(2,1)S(1)} %copy-done.2, f32[27,64,256]{2,1,0:T(8,128)S(1)} %copy-done.9, f32[27,64,256]{2,1,0:T(8,128)} %get-tuple-element.12.s1_ref, f32[8,64,256]{2,1,0:T(8,128)S(1)} %copy-done.13, f32[8,64,256]{2,1,0:T(8,128)S(1)} %copy-done.12), custom_call_target="tpu_custom_call" | custom-call | flops 6000000000 | bytes 20971520 | tf_op jit(solution)/shard_map/beams/pallas_call | solution.py:205
  174.7 12.0 %beams.3 = bf16[1,27,64,128]{3,2,1,0:T(8,128)(2,1)S(1)} custom-call(bf16[8,1,27,16,256]{4,3,2,1,0:T(8,128)(2,1)S(1)} %copy-done.3, f32[27,64,256]{2,1,0:T(8,128)S(1)} %copy-done.9, f32[27,64,256]{2,1,0:T(8,128)} %get-tuple-element.12.s1_ref, f32[8,64,256]{2,1,0:T(8,128)S(1)} %copy-done.10, f32[8,64,256]{2,1,0:T(8,128)S(1)} %copy-done.11), custom_call_target="tpu_custom_call" | custom-call | flops 6000000000 | bytes 20971520 | tf_op jit(solution)/shard_map/beams/pallas_call | solution.py:205
  186.7 1.1 pad_maximum_fusion
  187.8 0.0 reduce-scatter.2.cloned.1.call-update
  187.8 1.7 left_side.2.left_ref
  189.5 2.0 copy-done.5
  191.6 2.2 copy-done.6
  193.7 8.3 %correlate.2 = bf16[8,1,2,256,128]{4,3,2,1,0:T(8,128)(2,1)} custom-call(f32[1]{0:T(128)} %get-tuple-element.15.scale_ref, bf16[1,8,512,432]{3,2,1,0:T(8,128)(2,1)S(1)} %copy-done.6, bf16[4,8,1,27,16,256]{5,4,3,2,1,0:T(8,128)(2,1)} %bitcast.22), custom_call_target="tpu_custom_call" | custom-call | tf_op jit(solution)/shard_map/correlate/pallas_call | solution.py:275
  202.0 5.9 %all-to-all-start.1 = ((bf16[8,2,256,128]{3,2,1,0:T(8,128)(2,1)}), bf16[8,2,256,128]{3,2,1,0:T(8,128)(2,1)S(1)}, u32[]{:S(2)}, u32[]{:S(2)}) async-start(bf16[8,2,256,128]{3,2,1,0:T(8,128)(2,1)} %bitcast.7), calls=%async_computation.1 | async-start | bytes 2097152 | tf_op jit(solution)/shard_map/all_to_all | solution.py:350
  207.9 0.1 dynamic-slice_convert_fusion
  208.0 5.4 %reduce-scatter.2.cloned.1.call-done = bf16[2,27,16,128]{3,2,1,0:T(8,128)(2,1)} async-done(((bf16[2,27,64,128]{3,2,1,0:T(8,128)(2,1)}), bf16[2,27,16,128]{3,2,1,0:T(8,128)(2,1)}) %reduce-scatter.2.cloned.1.call-update) | async-done | bytes 221200 | tf_op jit(solution)/shard_map/reduce_scatter | solution.py:358
  213.3 1.7 convert_multiply_fusion
  215.1 1.6 copy.20
  216.7 0.2 bitcast_reduce_fusion
  216.9 0.1 reshape.51
  217.0 0.6 multiply_multiply_fusion
  217.6 15.1 %all-to-all-done.1.refs_0_ = bf16[8,2,256,128]{3,2,1,0:T(8,128)(2,1)S(1)} async-done(((bf16[8,2,256,128]{3,2,1,0:T(8,128)(2,1)}), bf16[8,2,256,128]{3,2,1,0:T(8,128)(2,1)S(1)}, u32[]{:S(2)}, u32[]{:S(2)}) %all-to-all-start.1) | async-done | bytes 1048608 | tf_op jit(solution)/shard_map/all_to_all | solution.py:350
  232.7 1.0 copy-done.15
  233.7 6.2 %widen.1 = f32[16,2,256,128]{3,2,1,0:T(8,128)} custom-call(bf16[8,2,256,128]{3,2,1,0:T(8,128)(2,1)} %copy-done.15, bf16[8,2,256,128]{3,2,1,0:T(8,128)(2,1)} %all-to-all-done.3.refs_1_), custom_call_target="tpu_custom_call" | custom-call | tf_op jit(solution)/shard_map/widen/pallas_call | solution.py:305
  (31 shorter events, 0.1 us)
Async XLA Ops:
  7.2 119.4 %copy-start = (s32[64,1024]{1,0:T(8,128)S(1)}, s32[64,1024]{1,0:T(8,128)}, u32[]{:S(2)}) copy-start(s32[64,1024]{1,0:T(8,128)} %param.10) | copy-start | bytes 786436
  7.2 136.6 %all-gather.7.cloned.1.call-start = ((), (), s32[]{:S(2)}) async-start(), calls=%async_computation.7 | async-start | bytes 8847360 | tf_op jit(solution)/shard_map/all_gather | solution.py:339
  9.0 3.8 %copy-start.14 = (f32[6,3456]{1,0:T(8,128)S(1)}, f32[6,3456]{1,0:T(8,128)}, u32[]{:S(2)}) copy-start(f32[6,3456]{1,0:T(8,128)} %taps_ref.1) | copy-start | bytes 248836
  80.4 111.1 %all-gather.5.cloned.1.call-start = ((), (), s32[]{:S(2)}) async-start(), calls=%async_computation.6 | async-start | bytes 8847360 | tf_op jit(solution)/shard_map/all_gather | solution.py:339
  124.9 0.7 copy-start.16
  131.8 8.0 %copy-start.3 = (bf16[8,1,27,16,256]{4,3,2,1,0:T(8,128)(2,1)S(1)}, bf16[8,1,27,16,256]{4,3,2,1,0:T(8,128)(2,1)}, u32[]{:S(2)}) copy-start(bf16[8,1,27,16,256]{4,3,2,1,0:T(8,128)(2,1)} %all_to_all.20.x_ref) | copy-start | bytes 5308420
  141.5 2.2 copy-start.7
  143.8 2.2 copy-start.8
  153.4 1.0 copy-start.4
  154.4 4.4 %copy-start.2 = (bf16[8,1,27,16,256]{4,3,2,1,0:T(8,128)(2,1)S(1)}, bf16[8,1,27,16,256]{4,3,2,1,0:T(8,128)(2,1)}, u32[]{:S(2)}) copy-start(bf16[8,1,27,16,256]{4,3,2,1,0:T(8,128)(2,1)} %all_to_all.21.x_ref) | copy-start | bytes 5308420
  154.4 47.6 %all-to-all-start.3 = ((bf16[8,2,256,128]{3,2,1,0:T(8,128)(2,1)}), bf16[8,2,256,128]{3,2,1,0:T(8,128)(2,1)}, u32[]{:S(2)}, u32[]{:S(2)}) async-start(bf16[8,2,256,128]{3,2,1,0:T(8,128)(2,1)} %bitcast.17), calls=%async_computation.3 | async-start | bytes 2097152 | tf_op jit(solution)/shard_map/all_to_all | solution.py:350
  158.8 54.5 %reduce-scatter.2.cloned.1.call-start = ((), (), s32[]{:S(2)}) async-start(), calls=%async_computation.5 | async-start | bytes 1105920 | tf_op jit(solution)/shard_map/reduce_scatter | solution.py:358
  158.9 1.5 copy-start.9
  160.3 1.0 copy-start.12
  161.4 1.0 copy-start.13
  162.4 12.2 %copy-start.10 = (f32[8,64,256]{2,1,0:T(8,128)S(1)}, f32[8,64,256]{2,1,0:T(8,128)}, u32[]{:S(2)}) copy-start(f32[8,64,256]{2,1,0:T(8,128)} %get-tuple-element.10.c2_ref) | copy-start | bytes 1572868
  162.4 12.2 %copy-start.11 = (f32[8,64,256]{2,1,0:T(8,128)S(1)}, f32[8,64,256]{2,1,0:T(8,128)}, u32[]{:S(2)}) copy-start(f32[8,64,256]{2,1,0:T(8,128)} %get-tuple-element.11.s2_ref) | copy-start | bytes 1572868
  189.5 2.0 copy-start.5
  191.6 2.2 copy-start.6
  202.0 30.7 %all-to-all-start.1 = ((bf16[8,2,256,128]{3,2,1,0:T(8,128)(2,1)}), bf16[8,2,256,128]{3,2,1,0:T(8,128)(2,1)S(1)}, u32[]{:S(2)}, u32[]{:S(2)}) async-start(bf16[8,2,256,128]{3,2,1,0:T(8,128)(2,1)} %bitcast.7), calls=%async_computation.1 | async-start | bytes 2097152 | tf_op jit(solution)/shard_map/all_to_all | solution.py:350
  217.0 22.9 %copy-start.1 = (s32[64,1024]{1,0:T(8,128)S(1)}, s32[64,1024]{1,0:T(8,128)}, u32[]{:S(2)}) copy-start(s32[64,1024]{1,0:T(8,128)} %param.10) | copy-start | bytes 786436
  232.7 1.0 copy-start.15
Sparse Core Ops, SparseCore 0:
  80.5 49.7 all-gather.6
  131.9 50.9 all-gather.4
  187.9 25.3 reduce-scatter.1

commit v3 on v2

--- a/solution.py
+++ b/solution.py
@@ -16,6 +16,7 @@
 R1 = 27
 R2 = 128
 LANES = 128
+PIECES = (14, 13)
 ROWS = 16
 
 
@@ -54,7 +55,7 @@
 
 
 def channelize_kernel(groups, per, local, x_ref, taps_ref, mat_ref, factor_ref, *rest):
-    out_refs, mid_ref = rest[:local], rest[local]
+    out_refs, mid_ref = rest[:-1], rest[-1]
     step = pl.program_id(0)
     block_rows = x_ref.shape[1]
 
@@ -95,7 +96,7 @@
     def _():
         factor = factor_ref[...]
 
-        def outer(k1, carry):
+        def outer(piece, start, k1, carry):
             res = lax.dot_general(
                 mat_ref[k1],
                 mid_ref[k1],
@@ -104,10 +105,15 @@
             )
             res = (res * factor).astype(jnp.bfloat16)
             for og in range(groups):
-                out_refs[og % local][og // local, k1] = res[og * 2 * per : (og + 1) * 2 * per]
+                out_refs[og % local * len(PIECES) + piece][og // local, k1 - start] = res[
+                    og * 2 * per : (og + 1) * 2 * per
+                ]
             return carry
 
-        lax.fori_loop(0, R1, outer, 0)
+        start = 0
+        for piece, size in enumerate(PIECES):
+            lax.fori_loop(start, start + size, functools.partial(outer, piece, start), 0)
+            start += size
 
 
 def transform_table(groups, per):
@@ -142,11 +148,13 @@
             pl.BlockSpec((1, inputs_dev), lambda i: (0, 0)),
         ],
         out_specs=[
-            pl.BlockSpec((groups // local, R1, 2 * per, inputs_dev), lambda i: (0, 0, 0, 0))
+            pl.BlockSpec((groups // local, size, 2 * per, inputs_dev), lambda i: (0, 0, 0, 0))
+            for size in PIECES
         ]
         * local,
         out_shape=[
-            jax.ShapeDtypeStruct((groups // local, R1, 2 * per, inputs_dev), jnp.bfloat16)
+            jax.ShapeDtypeStruct((groups // local, size, 2 * per, inputs_dev), jnp.bfloat16)
+            for size in PIECES
         ]
         * local,
         scratch_shapes=[pltpu.VMEM((R1, inputs_dev, 2 * R2), jnp.bfloat16)],
@@ -155,24 +163,32 @@
     )(x, filter_taps, table, factor)
 
 
-def beam_kernel(per, x_ref, c1_ref, s1_ref, c2_ref, s2_ref, out_ref, w_ref):
-    spec_count = x_ref.shape[0]
-    inputs_dev = x_ref.shape[-1]
-    beams = c1_ref.shape[1]
+def beam_kernel(per, base_ref, *refs):
+    x_refs, (out_ref, w_ref, step_ref) = refs[: len(PIECES)], refs[len(PIECES) :]
+    spec_count = x_refs[0].shape[0]
+    inputs_dev = x_refs[0].shape[-1]
+    beams = base_ref.shape[1]
     cols = spec_count * 2 * per
     lane = lax.broadcasted_iota(jnp.int32, (beams, cols), 1)
     within = lane % per
     is_real = (lane % (2 * per)) < per
 
-    def one(k1, carry):
-        c1, s1 = c1_ref[k1], s1_ref[k1]
+    c2, s2 = base_ref[4], base_ref[5]
+    for q in range(per):
+        step_ref[2 * q], step_ref[2 * q + 1] = c2, s2
+        c2, s2 = cmul((c2, s2), (base_ref[2], base_ref[3]))
+    step_ref[2 * per] = jnp.ones((beams, inputs_dev), jnp.float32)
+    step_ref[2 * per + 1] = jnp.zeros((beams, inputs_dev), jnp.float32)
+
+    def one(x_ref, start, k1, carry):
+        c1, s1 = step_ref[2 * per], step_ref[2 * per + 1]
         for q in range(per):
-            c2, s2 = c2_ref[q], s2_ref[q]
-            w_ref[q * 2 * beams : q * 2 * beams + beams] = (c1 * c2 - s1 * s2).astype(jnp.bfloat16)
-            w_ref[q * 2 * beams + beams : (q + 1) * 2 * beams] = (s1 * c2 + c1 * s2).astype(
-                jnp.bfloat16
-            )
-        x = x_ref[:, 0, k1].reshape(cols, inputs_dev)
+            cos, sin = cmul((c1, s1), (step_ref[2 * q], step_ref[2 * q + 1]))
+            w_ref[q * 2 * beams : q * 2 * beams + beams] = cos.astype(jnp.bfloat16)
+            w_ref[q * 2 * beams + beams : (q + 1) * 2 * beams] = sin.astype(jnp.bfloat16)
+        c1, s1 = cmul((c1, s1), (base_ref[0], base_ref[1]))
+        step_ref[2 * per], step_ref[2 * per + 1] = c1, s1
+        x = x_ref[:, 0, k1 - start].reshape(cols, inputs_dev)
         prod = lax.dot_general(
             w_ref[...], x, (((1,), (1,)), ((), ())), preferred_element_type=jnp.float32
         )
@@ -189,108 +205,105 @@
         out_ref[0, k1] = (with_cos + jnp.where(is_real, ahead, -behind)).astype(jnp.bfloat16)
         return carry
 
-    lax.fori_loop(0, R1, one, 0)
-
-
-def beams_of(turned, delays, k2_start, local, per):
-    spec_count, _, _, _, inputs_dev = turned.shape
+    start = 0
+    for x_ref, size in zip(x_refs, PIECES):
+        lax.fori_loop(start, start + size, functools.partial(one, x_ref, start), 0)
+        start += size
+
+
+def beams_of(turned, delays, k2_start, per):
+    spec_count, inputs_dev = turned[0].shape[0], turned[0].shape[-1]
     beams = delays.shape[0]
     cols = spec_count * 2 * per
-    ids1 = jnp.arange(R1, dtype=jnp.int32)[:, None, None]
-    ids2 = (k2_start + jnp.arange(local * per, dtype=jnp.int32))[:, None, None]
-    ang1 = (delays[None] * ids1 % FINE).astype(jnp.float32) * (2.0 * math.pi / FINE)
-    ang2 = (delays[None] * ids2 % R2).astype(jnp.float32) * (2.0 * math.pi / R2)
-    small = pl.BlockSpec((R1, beams, inputs_dev), lambda o: (0, 0, 0))
-    large = pl.BlockSpec((per, beams, inputs_dev), lambda o: (o, 0, 0))
+    turns = jnp.stack([delays, delays * R1 % FINE, (delays * k2_start % R2) * R1])
+    angles = turns.astype(jnp.float32) * (2.0 * math.pi / FINE)
+    base = jnp.stack([jnp.cos(angles), jnp.sin(angles)], axis=1)
+    base = base.reshape(6, beams, inputs_dev)
     return pl.pallas_call(
         functools.partial(beam_kernel, per),
-        grid=(local,),
-        in_specs=[
-            pl.BlockSpec((spec_count, 1, R1, 2 * per, inputs_dev), lambda o: (0, o, 0, 0, 0)),
-            small,
-            small,
-            large,
-            large,
+        out_shape=jax.ShapeDtypeStruct((1, R1, beams, cols), jnp.bfloat16),
+        scratch_shapes=[
+            pltpu.VMEM((per * 2 * beams, inputs_dev), jnp.bfloat16),
+            pltpu.VMEM((2 * per + 2, beams, inputs_dev), jnp.float32),
         ],
-        out_specs=pl.BlockSpec((1, R1, beams, cols), lambda o: (o, 0, 0, 0)),
-        out_shape=jax.ShapeDtypeStruct((local, R1, beams, cols), jnp.bfloat16),
-        scratch_shapes=[pltpu.VMEM((per * 2 * beams, inputs_dev), jnp.bfloat16)],
-        compiler_params=pltpu.CompilerParams(vmem_limit_bytes=48 << 20),
+        compiler_params=pltpu.CompilerParams(vmem_limit_bytes=32 << 20),
         cost_estimate=pl.CostEstimate(
-            flops=int(6e9), bytes_accessed=20 << 20, transcendentals=0
+            flops=int(6e9), bytes_accessed=10 << 20, transcendentals=0
         ),
         name="beams",
-    )(turned, jnp.cos(ang1), jnp.sin(ang1), jnp.cos(ang2), jnp.sin(ang2))
+    )(base, *turned)
 
 
 def left_kernel(per, x_ref, out_ref):
     inputs_dev = x_ref.shape[-1]
-    depth = R1 * 2 * per
+    size = x_ref.shape[2]
+    depth = size * 2 * per
     x = x_ref[0, 0].reshape(depth, inputs_dev).astype(jnp.float32)
-    pairs = x.reshape(R1, 2, per, inputs_dev)
+    pairs = x.reshape(size, 2, per, inputs_dev)
     turned = jnp.concatenate([pairs[:, 1:], -pairs[:, :1]], axis=1).reshape(depth, inputs_dev)
     out_ref[0, 0, 0:inputs_dev] = x.T.astype(jnp.bfloat16)
     out_ref[0, 0, inputs_dev : 2 * inputs_dev] = turned.T.astype(jnp.bfloat16)
 
 
 def left_of(turned, per):
-    spec_count, local, _, _, inputs_dev = turned.shape
-    depth = R1 * 2 * per
+    spec_count, local, size, _, inputs_dev = turned.shape
+    depth = size * 2 * per
     return pl.pallas_call(
         functools.partial(left_kernel, per),
         grid=(local, spec_count),
         in_specs=[
-            pl.BlockSpec((1, 1, R1, 2 * per, inputs_dev), lambda o, s: (s, o, 0, 0, 0)),
+            pl.BlockSpec((1, 1, size, 2 * per, inputs_dev), lambda o, s: (s, o, 0, 0, 0)),
         ],
         out_specs=pl.BlockSpec((1, 1, 2 * inputs_dev, depth), lambda o, s: (o, s, 0, 0)),
         out_shape=jax.ShapeDtypeStruct((local, spec_count, 2 * inputs_dev, depth), jnp.bfloat16),
         compiler_params=pltpu.CompilerParams(vmem_limit_bytes=32 << 20),
-        cost_estimate=pl.CostEstimate(flops=int(2e9), bytes_accessed=10 << 20, transcendentals=0),
+        cost_estimate=pl.CostEstimate(flops=int(5e8), bytes_accessed=3 << 20, transcendentals=0),
         name="left_side",
     )(turned)
 
 
-def correlate_kernel(scale_ref, left_ref, right_ref, out_ref):
-    inputs_dev = right_ref.shape[-1]
-    spec_count, depth = left_ref.shape[1], left_ref.shape[3]
+def correlate_kernel(scale_ref, *refs):
+    count = len(PIECES)
+    lefts, rights, out_ref = refs[:count], refs[count : 2 * count], refs[-1]
+    inputs_dev = rights[0].shape[-1]
+    spec_count = lefts[0].shape[1]
     total = jnp.zeros((2 * inputs_dev, inputs_dev), jnp.float32)
-    for s in range(spec_count):
-        total = total + jnp.dot(
-            left_ref[0, s],
-            right_ref[0, s, 0].reshape(depth, inputs_dev),
-            preferred_element_type=jnp.float32,
-        )
-    total = (total * scale_ref[pl.program_id(0)]).astype(jnp.bfloat16)
+    for left_ref, right_ref in zip(lefts, rights):
+        depth = left_ref.shape[3]
+        for s in range(spec_count):
+            total = total + jnp.dot(
+                left_ref[0, s],
+                right_ref[0, s, 0].reshape(depth, inputs_dev),
+                preferred_element_type=jnp.float32,
+            )
+    total = (total * scale_ref[0]).astype(jnp.bfloat16)
     for part in range(2):
         for h in range(inputs_dev // LANES):
-            out_ref[h, 0, part] = total[
+            out_ref[h, part] = total[
                 part * inputs_dev : (part + 1) * inputs_dev, h * LANES : (h + 1) * LANES
             ]
 
 
-def correlate(scale, left, right):
-    count, spec_count, local, _, rows, inputs_dev = right.shape
+def correlate(scale, lefts, rights):
+    count, spec_count, _, _, rows, inputs_dev = rights[0].shape
     halves = inputs_dev // LANES
-    depth = left.shape[3]
     return pl.pallas_call(
         correlate_kernel,
-        grid=(local, count),
-        in_specs=[
-            pl.BlockSpec(memory_space=pltpu.SMEM),
-            pl.BlockSpec((1, spec_count, 2 * inputs_dev, depth), lambda o, j: (o, 0, 0, 0)),
-            pl.BlockSpec(
-                (1, spec_count, 1, R1, rows, inputs_dev), lambda o, j: (j, 0, o, 0, 0, 0)
-            ),
+        grid=(count,),
+        in_specs=[pl.BlockSpec(memory_space=pltpu.SMEM)]
+        + [pl.BlockSpec(left.shape, lambda j: (0, 0, 0, 0)) for left in lefts]
+        + [
+            pl.BlockSpec((1,) + right.shape[1:], lambda j: (j, 0, 0, 0, 0, 0))
+            for right in rights
         ],
-        out_specs=pl.BlockSpec(
-            (halves, 1, 2, inputs_dev, LANES), lambda o, j: (j, o, 0, 0, 0)
+        out_specs=pl.BlockSpec((halves, 2, inputs_dev, LANES), lambda j: (j, 0, 0, 0)),
+        out_shape=jax.ShapeDtypeStruct((count * halves, 2, inputs_dev, LANES), jnp.bfloat16),
+        compiler_params=pltpu.CompilerParams(vmem_limit_bytes=48 << 20),
+        cost_estimate=pl.CostEstimate(
+            flops=int(7e9), bytes_accessed=12 << 20, transcendentals=0
         ),
-        out_shape=jax.ShapeDtypeStruct(
-            (count * halves, local, 2, inputs_dev, LANES), jnp.bfloat16
-        ),
-        compiler_params=pltpu.CompilerParams(vmem_limit_bytes=48 << 20),
         name="correlate",
-    )(scale, left, right)
+    )(scale, *lefts, *rights)
 
 
 def widen_kernel(*refs):
@@ -335,14 +348,13 @@
 
     turned, gathered, volts, vis = [], [], [], []
     for o in range(local):
-        turned.append(lax.all_to_all(spectra[o][:, None], "tm", 0, 0, tiled=True))
-        gathered.append(lax.all_gather(turned[o], "stn", axis=0, tiled=False))
+        own = spectra[o * len(PIECES) : (o + 1) * len(PIECES)]
+        turned.append([lax.all_to_all(x[:, None], "tm", 0, 0, tiled=True) for x in own])
+        gathered.append([lax.all_gather(x, "stn", axis=0, tiled=False) for x in turned[o]])
     for o in range(local):
-        left = left_of(turned[o], per)
-        volts.append(
-            beams_of(turned[o], own_delays, tm_index * k2_dev + o * per, 1, per)
-        )
-        parts = correlate(scale[o : o + 1], left, gathered[o])
+        lefts = [left_of(x, per) for x in turned[o]]
+        volts.append(beams_of(turned[o], own_delays, tm_index * k2_dev + o * per, per))
+        parts = correlate(scale[o : o + 1], lefts, gathered[o])
         if cols != LANES:
             parts = parts.reshape(-1, 2, inputs_dev, LANES // cols, cols)
             parts = parts.transpose(0, 3, 1, 2, 4)

time: 248 us -> 248 us (level)
  blocking collectives: 92.9 us -> 106 us
  other arithmetic: 22.4 us -> 12.5 us
    sin x2 -> x0, other arithmetic: 13.2 us -> none  [the longest x1 7.99 us: beams_of(): jnp.sin(ang1)]
    all_to_all x2 -> x4, blocking collectives: 92.9 us -> 106 us  [on_device(): lax.all_to_all(x[:, None], 'tm', 0, 0, tiled=True)]
    pallas_call x4, Pallas kernels: 39.9 us -> 36.7 us  [the longest x2 21.2 us: beams_of(): pl.pallas_call(functools.partial(beam_kernel, per), out_shape=jax.ShapeDt...]
    another operation x0 -> x3, other arithmetic: none -> 2.5 us  [the longest x2 1.56 us: beams_of(): base = jnp.stack([jnp.cos(angles), jnp.sin(angles)], axis=1)]
    unnamed x34 -> x36, local copies, waits for them, and re-layouts: 14.9 us -> 14.7 us
  transfers between devices with their start and end apart: 5 -> 7, of which waited for: 2 -> 2; matrix products, arithmetic and copies ran while one was open for 8% -> 4% of each run, Pallas kernels for 18% -> 17%
where the time goes in v3:
time: 248 us; the launch traced here: 247 us
  blocking collectives  106 us (43%)
  Pallas kernels  66.7 us (27%)
  waiting for transfers between devices  19.8 us (8%)
  local copies, waits for them, and re-layouts  17.4 us (7%)
  between operations  14 us (6%)
  other arithmetic  12.5 us (5%)
  starting transfers between devices  10.3 us (4%)
    all_to_all x4, blocking collectives, on_device(): lax.all_to_all(x[:, None], 'tm', 0, 0, tiled=True)  106 us
    pallas_call x2, Pallas kernels, beams_of(): pl.pallas_call(functools.partial(beam_kernel, per), out_shape=jax.ShapeDt...  21.2 us
    pallas_call x1, Pallas kernels, channelize(): pl.pallas_call(functools.partial(channelize_kernel, groups, per, local),...  19.2 us
    pallas_call x2, Pallas kernels, correlate(): pl.pallas_call(correlate_kernel, grid=(count,), in_specs=[pl.BlockSpec(me...  15.5 us
    unnamed x36, local copies, waits for them, and re-layouts  14.7 us
    all_to_all x2, waiting for transfers between devices, on_device(): vis.append(lax.all_to_all(parts, 'tm', 0, 0, tiled=True))  14.2 us
    all_to_all x2, starting transfers between devices, on_device(): vis.append(lax.all_to_all(parts, 'tm', 0, 0, tiled=True))  10.1 us
    pallas_call x1, Pallas kernels, widen(): pl.pallas_call(widen_kernel, grid=(count,), in_specs=[pl.BlockSpec((1, 2,...  6.19 us
  transfers between devices with their start and end apart: 7, of which 2 were waited for; matrix products, arithmetic and copies ran while one was open for 4% of the time, Pallas kernels for 17%

profile of v3, /device:TPU:0, one launch (start us, length us, event | category | flops | bytes accessed | tf_op | source)
XLA Modules:
  0.0 246.9 jit_solution(1609561768464252833)
XLA Ops:
  7.2 0.7 convert_element_type.62
  7.9 0.2 convert_element_type.63
  8.2 0.1 copy.23
  8.3 0.7 convert_multiply_fusion.1
  9.0 3.8 %broadcast_multiply_fusion.mat_ref = bf16[27,256,256]{2,1,0:T(8,128)(2,1)} fusion(bf16[27,256,256]{2,1,0:T(8,128)(2,1)} %constant.78.clone, bf16[27,256]{1,0:T(8,128)(2,1)S(1)} %copy.23), kind=kLoop, calls=%fused_computation.1 | loop fusion | flops 1769472 | bytes 7091712 | tf_op jit(solution)/shard_map/mul | solution.py:138
  12.8 19.2 %channelize.1 = (bf16[8,14,16,256]{3,2,1,0:T(8,128)(2,1)S(1)}, bf16[8,13,16,256]{3,2,1,0:T(8,128)(2,1)S(1)}, bf16[8,14,16,256]{3,2,1,0:T(8,128)(2,1)S(1)}, bf16[8,13,16,256]{3,2,1,0:T(8,128)(2,1)S(1)}) custom-call(bf16[2,256,20736]{2,1,0:T(8,128)(2,1)} %bitcast.36, f32[6,3456]{1,0:T(8,128)S(1)} %copy-done.15, ...), custom_call_target="tpu_custom_call" | custom-call | tf_op jit(solution)/shard_map/channelize/pallas_call | solution.py:141
  32.0 29.4 %all_to_all.30.x_ref.refs_1_ = bf16[8,1,13,16,256]{4,3,2,1,0:T(8,128)(2,1)} all-to-all(bf16[8,1,13,16,256]{4,3,2,1,0:T(8,128)(2,1)S(1)} %bitcast.32), channel_id=1, replica_groups=mesh['stn'=4,'tm'=8] {'tm'}, dimensions={0} | all-to-all | bytes 1703936 | tf_op jit(solution)/shard_map/all_to_all | solution.py:352
  61.4 26.0 %all_to_all.31.x_ref.refs_0_ = bf16[8,1,14,16,256]{4,3,2,1,0:T(8,128)(2,1)} all-to-all(bf16[8,1,14,16,256]{4,3,2,1,0:T(8,128)(2,1)S(1)} %bitcast.30), channel_id=1, replica_groups=mesh['stn'=4,'tm'=8] {'tm'}, dimensions={0} | all-to-all | bytes 1835008 | tf_op jit(solution)/shard_map/all_to_all | solution.py:352
  87.5 24.8 %all_to_all.32.x_ref.refs_1_ = bf16[8,1,13,16,256]{4,3,2,1,0:T(8,128)(2,1)} all-to-all(bf16[8,1,13,16,256]{4,3,2,1,0:T(8,128)(2,1)S(1)} %bitcast.31), channel_id=1, replica_groups=mesh['stn'=4,'tm'=8] {'tm'}, dimensions={0} | all-to-all | bytes 1703936 | tf_op jit(solution)/shard_map/all_to_all | solution.py:352
  112.4 25.8 %all_to_all.33.x_ref.refs_0_ = bf16[8,1,14,16,256]{4,3,2,1,0:T(8,128)(2,1)} all-to-all(bf16[8,1,14,16,256]{4,3,2,1,0:T(8,128)(2,1)S(1)} %bitcast.29), channel_id=1, replica_groups=mesh['stn'=4,'tm'=8] {'tm'}, dimensions={0} | all-to-all | bytes 1835008 | tf_op jit(solution)/shard_map/all_to_all | solution.py:352
  138.3 0.1 reshape.193
  138.4 0.1 reduce_sum.18
  138.6 0.1 multiply_divide_fusion
  138.6 0.6 fusion.13
  139.2 0.9 fusion.9
  140.2 1.0 fusion.5
  141.2 0.8 pad_maximum_fusion.1
  142.0 0.8 pad_maximum_fusion.2
  142.8 1.2 left_side.7.refs_1_
  143.9 1.3 copy-done.8
  145.3 1.2 left_side.5.refs_1_
  146.4 1.3 copy-done.4
  147.8 1.2 left_side.6.refs_0_
  148.9 1.3 copy-done.10
  150.3 1.6 copy-done.9
  151.8 1.6 copy-done.11
  153.4 7.4 %correlate.3 = bf16[8,2,256,128]{3,2,1,0:T(8,128)(2,1)S(1)} custom-call(f32[1]{0:T(128)} %get-tuple-element.20.scale_ref, bf16[1,8,512,224]{3,2,1,0:T(8,128)(2,1)S(1)} %copy-done.11, bf16[1,8,512,208]{3,2,1,0:T(8,128)(2,1)S(1)} %copy-done.9, bf16[4,8,1,14,16,256]{5,4,3,2,1,0:T(8,128)(2,1)} %bitcast.41, bf16[4,8,1,13,16,256]{5,4,3,2,1,0:T(8,128)(2,1)} %bitcast.43), custom_call_target="tpu_custom_call" | custom-call | flops 7000000000 | bytes 12582912 | tf_op jit(solution)/shard_map/correlate/pallas_call | solution.py:290
  160.9 1.0 copy-done.12
  161.9 4.3 %all-to-all-start.5 = ((bf16[8,2,256,128]{3,2,1,0:T(8,128)(2,1)}), bf16[8,2,256,128]{3,2,1,0:T(8,128)(2,1)}, u32[]{:S(2)}, u32[]{:S(2)}) async-start(bf16[8,2,256,128]{3,2,1,0:T(8,128)(2,1)} %copy-done.12), calls=%async_computation.5 | async-start | bytes 2097152 | tf_op jit(solution)/shard_map/all_to_all | solution.py:362
  166.2 1.0 copy-done.13
  167.2 10.6 %beams.2 = bf16[1,27,64,128]{3,2,1,0:T(8,128)(2,1)S(1)} custom-call(f32[6,64,256]{2,1,0:T(8,128)S(1)} %bitcast.33, bf16[8,1,14,16,256]{4,3,2,1,0:T(8,128)(2,1)S(1)} %copy-done.1, bf16[8,1,13,16,256]{4,3,2,1,0:T(8,128)(2,1)S(1)} %copy-done.3), custom_call_target="tpu_custom_call" | custom-call | flops 6000000000 | bytes 10485760 | tf_op jit(solution)/shard_map/beams/pallas_call | solution.py:222
  177.8 10.6 %beams.3 = bf16[1,27,64,128]{3,2,1,0:T(8,128)(2,1)S(1)} custom-call(f32[6,64,256]{2,1,0:T(8,128)S(1)} %bitcast.34, bf16[8,1,14,16,256]{4,3,2,1,0:T(8,128)(2,1)S(1)} %copy-done, bf16[8,1,13,16,256]{4,3,2,1,0:T(8,128)(2,1)S(1)} %copy-done.2), custom_call_target="tpu_custom_call" | custom-call | flops 6000000000 | bytes 10485760 | tf_op jit(solution)/shard_map/beams/pallas_call | solution.py:222
  188.5 1.0 pad_maximum_fusion
  189.5 1.2 left_side.4.refs_0_
  190.7 1.3 copy-done.6
  192.0 1.6 copy-done.5
  193.6 1.6 copy-done.7
  195.2 8.1 %correlate.2 = bf16[8,2,256,128]{3,2,1,0:T(8,128)(2,1)} custom-call(f32[1]{0:T(128)} %get-tuple-element.21.scale_ref, bf16[1,8,512,224]{3,2,1,0:T(8,128)(2,1)S(1)} %copy-done.7, bf16[1,8,512,208]{3,2,1,0:T(8,128)(2,1)S(1)} %copy-done.5, bf16[4,8,1,14,16,256]{5,4,3,2,1,0:T(8,128)(2,1)} %bitcast.40, bf16[4,8,1,13,16,256]{5,4,3,2,1,0:T(8,128)(2,1)} %bitcast.42), custom_call_target="tpu_custom_call" | custom-call | flops 7000000000 | bytes 12582912 | tf_op jit(solution)/shard_map/correlate/pallas_call | solution.py:290
  203.3 5.9 %all-to-all-start.2 = ((bf16[8,2,256,128]{3,2,1,0:T(8,128)(2,1)}), bf16[8,2,256,128]{3,2,1,0:T(8,128)(2,1)S(1)}, u32[]{:S(2)}, u32[]{:S(2)}) async-start(bf16[8,2,256,128]{3,2,1,0:T(8,128)(2,1)} %correlate.2), calls=%async_computation.2 | async-start | bytes 2097152 | tf_op jit(solution)/shard_map/all_to_all | solution.py:362
  209.2 5.6 %reduce-scatter.2.cloned.1.call-done = bf16[2,27,16,128]{3,2,1,0:T(8,128)(2,1)} async-done(((bf16[2,27,64,128]{3,2,1,0:T(8,128)(2,1)}), bf16[2,27,16,128]{3,2,1,0:T(8,128)(2,1)}) %reduce-scatter.2.cloned.1.call-update) | async-done | bytes 221200 | tf_op jit(solution)/shard_map/reduce_scatter | solution.py:370
  214.7 1.7 convert_multiply_fusion
  216.5 1.6 copy.24
  218.1 0.2 bitcast_reduce_fusion
  218.3 0.1 reshape.198
  218.4 0.6 multiply_multiply_fusion
  219.0 14.2 %all-to-all-done.2.refs_0_ = bf16[8,2,256,128]{3,2,1,0:T(8,128)(2,1)S(1)} async-done(((bf16[8,2,256,128]{3,2,1,0:T(8,128)(2,1)}), bf16[8,2,256,128]{3,2,1,0:T(8,128)(2,1)S(1)}, u32[]{:S(2)}, u32[]{:S(2)}) %all-to-all-start.2) | async-done | bytes 1048608 | tf_op jit(solution)/shard_map/all_to_all | solution.py:362
  233.2 1.0 copy-done.16
  234.2 6.2 %widen.1 = f32[16,2,256,128]{3,2,1,0:T(8,128)} custom-call(bf16[8,2,256,128]{3,2,1,0:T(8,128)(2,1)} %copy-done.16, bf16[8,2,256,128]{3,2,1,0:T(8,128)(2,1)} %all-to-all-done.5.refs_1_), custom_call_target="tpu_custom_call" | custom-call | tf_op jit(solution)/shard_map/widen/pallas_call | solution.py:318
  (43 shorter events, 0.4 us)
Async XLA Ops:
  7.2 143.1 %all-gather.15.cloned.1.call-start = ((), (), s32[]{:S(2)}) async-start(), calls=%async_computation.11 | async-start | bytes 4259840 | tf_op jit(solution)/shard_map/all_gather | solution.py:353
  9.0 3.8 %copy-start.15 = (f32[6,3456]{1,0:T(8,128)S(1)}, f32[6,3456]{1,0:T(8,128)}, u32[]{:S(2)}) copy-start(f32[6,3456]{1,0:T(8,128)} %taps_ref.1) | copy-start | bytes 248836
  61.4 88.9 %all-gather.13.cloned.1.call-start = ((), (), s32[]{:S(2)}) async-start(), calls=%async_computation.10 | async-start | bytes 4587520 | tf_op jit(solution)/shard_map/all_gather | solution.py:353
  87.5 50.9 %copy-start.17 = (s32[3456]{0:T(1024)S(1)}, s32[3456]{0:T(1024)}, u32[]{:S(2)}) copy-start(s32[3456]{0:T(1024)} %param.9) | copy-start | bytes 41476
  87.5 104.5 %all-gather.11.cloned.1.call-start = ((), (), s32[]{:S(2)}) async-start(), calls=%async_computation.9 | async-start | bytes 4259840 | tf_op jit(solution)/shard_map/all_gather | solution.py:353
  112.4 30.4 %copy-start.2 = (bf16[8,1,13,16,256]{4,3,2,1,0:T(8,128)(2,1)S(1)}, bf16[8,1,13,16,256]{4,3,2,1,0:T(8,128)(2,1)}, u32[]{:S(2)}) copy-start(bf16[8,1,13,16,256]{4,3,2,1,0:T(8,128)(2,1)} %all_to_all.30.x_ref.refs_1_) | copy-start | bytes 2555908
  112.4 79.6 %all-gather.9.cloned.1.call-start = ((), (), s32[]{:S(2)}) async-start(), calls=%async_computation.8 | async-start | bytes 4587520 | tf_op jit(solution)/shard_map/all_gather | solution.py:353
  138.3 7.0 %copy-start.3 = (bf16[8,1,13,16,256]{4,3,2,1,0:T(8,128)(2,1)S(1)}, bf16[8,1,13,16,256]{4,3,2,1,0:T(8,128)(2,1)}, u32[]{:S(2)}) copy-start(bf16[8,1,13,16,256]{4,3,2,1,0:T(8,128)(2,1)} %all_to_all.32.x_ref.refs_1_) | copy-start | bytes 2555908
  142.0 5.8 %copy-start = (bf16[8,1,14,16,256]{4,3,2,1,0:T(8,128)(2,1)S(1)}, bf16[8,1,14,16,256]{4,3,2,1,0:T(8,128)(2,1)}, u32[]{:S(2)}) copy-start(bf16[8,1,14,16,256]{4,3,2,1,0:T(8,128)(2,1)} %all_to_all.31.x_ref.refs_0_) | copy-start | bytes 2752516
  143.9 1.3 copy-start.8
  146.4 1.3 copy-start.4
  148.9 1.3 copy-start.10
  150.3 1.6 copy-start.9
  151.8 1.6 copy-start.11
  153.4 12.8 %copy-start.1 = (bf16[8,1,14,16,256]{4,3,2,1,0:T(8,128)(2,1)S(1)}, bf16[8,1,14,16,256]{4,3,2,1,0:T(8,128)(2,1)}, u32[]{:S(2)}) copy-start(bf16[8,1,14,16,256]{4,3,2,1,0:T(8,128)(2,1)} %all_to_all.33.x_ref.refs_0_) | copy-start | bytes 2752516
  160.9 1.0 copy-start.12
  161.9 41.4 %all-to-all-start.5 = ((bf16[8,2,256,128]{3,2,1,0:T(8,128)(2,1)}), bf16[8,2,256,128]{3,2,1,0:T(8,128)(2,1)}, u32[]{:S(2)}, u32[]{:S(2)}) async-start(bf16[8,2,256,128]{3,2,1,0:T(8,128)(2,1)} %copy-done.12), calls=%async_computation.5 | async-start | bytes 2097152 | tf_op jit(solution)/shard_map/all_to_all | solution.py:362
  166.2 48.6 %reduce-scatter.2.cloned.1.call-start = ((), (), s32[]{:S(2)}) async-start(), calls=%async_computation.7 | async-start | bytes 1105920 | tf_op jit(solution)/shard_map/reduce_scatter | solution.py:370
  166.2 1.0 copy-start.13
  167.2 10.6 %copy-start.14 = (f32[3,2,64,256]{3,2,1,0:T(8,128)S(1)}, f32[3,2,64,256]{3,2,1,0:T(8,128)}, u32[]{:S(2)}) copy-start(f32[3,2,64,256]{3,2,1,0:T(8,128)} %pad_maximum_fusion.2) | copy-start | bytes 1179652
  190.7 1.3 copy-start.6
  192.0 1.6 copy-start.5
  193.6 1.6 copy-start.7
  203.3 30.0 %all-to-all-start.2 = ((bf16[8,2,256,128]{3,2,1,0:T(8,128)(2,1)}), bf16[8,2,256,128]{3,2,1,0:T(8,128)(2,1)S(1)}, u32[]{:S(2)}, u32[]{:S(2)}) async-start(bf16[8,2,256,128]{3,2,1,0:T(8,128)(2,1)} %correlate.2), calls=%async_computation.2 | async-start | bytes 2097152 | tf_op jit(solution)/shard_map/all_to_all | solution.py:362
  233.2 1.0 copy-start.16
Sparse Core Ops, SparseCore 0:
  61.5 28.3 all-gather.14
  91.5 31.5 all-gather.12
  124.6 30.0 all-gather.10
  156.1 31.4 all-gather.8
  190.0 24.6 reduce-scatter.1
